TPU v7x, 256 devices: a whole 4x4x8 slice. The times are simulated.
256 devices in a mesh: blk: 64 (over z, y_hi, x), rep: 4 (over y_lo, core).
Axes of the slice: x: 4, y: 4 (y_hi: 2, y_lo: 2; y = y_hi * 2 + y_lo), z: 8, core: 2. Of those that a mesh axis runs over, the one named last changes fastest.
Arguments:
- audio_emb: bfloat16 [131072, 1280], P(('blk', 'rep')), may hold values from -6 to 6
- text_emb: bfloat16 [131072, 1024], P(('blk', 'rep')), may hold values from -180 to 180
- proj_weight: bfloat16 [1280, 1024], replicated, may hold values from -0.15625 to 0.15625
- pair_index: int32 [256, 512], P(('blk', 'rep')), may hold values from 0 to 511, each once within a row
Outputs:
- row_loss: float32 [131072], P(('blk', 'rep'))
- text_grad: bfloat16 [131072, 1024], P(('blk', 'rep'))
- proj_grad: float32 [1280, 1024], replicated
Inputs may be any that keep to these rules, and one draw needn't show every extreme that they name: Each device's row of pair_index is a permutation of 0 .. 511.
All inputs are finite; a program needn't handle non-finite values.
Results may differ from a plain program's by a relative error of at most 0.009.
The roundings to bfloat16 on the way count: a program that leaves them out, or rounds other values in their place, can miss the bound.
Values may be sent and summed in bfloat16 or wider, within the bound.
A program may use at most 128 MiB of HBM per device.

v0:
```python
import math

import jax
import jax.numpy as jnp
from jax import lax
from jax.sharding import PartitionSpec as P

REACH = 3


def passed_along(shard, axis, by):
    length = lax.axis_size(axis)
    return lax.ppermute(shard, axis, [(i, (i + by) % length) for i in range(length)])


def on_device(audio_emb, text_emb, proj_weight, pair_index):
    width = text_emb.shape[1]
    rows = text_emb.shape[0]
    scale = 4.0 / math.sqrt(width)
    proj = jnp.dot(audio_emb, proj_weight, preferred_element_type=jnp.float32).astype(jnp.bfloat16)
    tiles = {0: text_emb}
    moving = passed_along(text_emb, "blk", REACH)
    tiles[-REACH] = moving
    for offset in range(-REACH + 1, REACH + 1):
        moving = passed_along(moving, "blk", -1)
        if offset != 0:
            tiles[offset] = moving
    offsets = list(range(-REACH, REACH + 1))
    columns = jnp.arange(rows, dtype=jnp.int32)
    onehot = (pair_index[0][:, None] == columns[None, :]).astype(jnp.float32)
    scores = {}
    for k in offsets:
        scores[k] = scale * lax.dot_general(
            proj, tiles[k], (((1,), (1,)), ((), ())), preferred_element_type=jnp.float32
        )
    top = jnp.max(jnp.stack([jnp.max(scores[k], axis=1) for k in offsets]), axis=0)
    total = sum((jnp.sum(jnp.exp(scores[k] - top[:, None]), axis=1) for k in offsets))
    lse = top + jnp.log(total)
    row_loss = lse - jnp.sum(scores[0] * onehot, axis=1)
    delta = jnp.zeros((rows, width), jnp.float32)
    shares = {}
    for k in offsets:
        prob = jnp.exp(scores[k] - lse[:, None])
        if k == 0:
            prob = prob - onehot
        weight = prob.astype(jnp.bfloat16)
        delta = delta + jnp.dot(weight, tiles[k], preferred_element_type=jnp.float32)
        shares[k] = scale * lax.dot_general(
            weight, proj, (((0,), (0,)), ((), ())), preferred_element_type=jnp.float32
        )
    proj_delta = (scale * delta).astype(jnp.bfloat16)
    text_acc = shares[0]
    for k in offsets:
        if k != 0:
            text_acc = text_acc + passed_along(shares[k], "blk", k)
    text_grad = text_acc.astype(jnp.bfloat16)
    term = lax.dot_general(
        audio_emb, proj_delta, (((0,), (0,)), ((), ())), preferred_element_type=jnp.float32
    )
    summed = lax.psum(term, ("blk", "rep"))
    proj_grad = summed / float(lax.axis_size("blk") * lax.axis_size("rep"))
    return (row_loss, text_grad, proj_grad)


def solution(mesh):
    return jax.shard_map(
        on_device,
        mesh=mesh,
        in_specs=(P(("blk", "rep"), None), P(("blk", "rep"), None), P(), P(("blk", "rep"), None)),
        out_specs=(P(("blk", "rep")), P(("blk", "rep"), None), P()),
        check_vma=False,
    )
```

profile of v0, /device:TPU:1, one launch (start us, length us, event | category | flops | bytes accessed | tf_op | source)
XLA Modules:
  0.0 740.9 jit_solution(1064982801779367074)
XLA Ops:
  7.2 3.4 collective-permute-start
  10.6 29.8 %collective-permute-done = bf16[512,1024]{1,0:T(8,128)(2,1)S(1)} collective-permute-done((bf16[512,1024]{1,0:T(8,128)(2,1)}, bf16[512,1024]{1,0:T(8,128)(2,1)S(1)}, u32[]{:S(2)}, u32[]{:S(2)}) %collective-permute-start) | collective-permute-done | bytes 1048608 | tf_op jit(solution)/shard_map/ppermute | solution.py:13
  40.4 3.6 collective-permute-start.1
  44.0 20.9 %collective-permute-done.1 = bf16[512,1024]{1,0:T(8,128)(2,1)S(1)} collective-permute-done((bf16[512,1024]{1,0:T(8,128)(2,1)S(1)}, bf16[512,1024]{1,0:T(8,128)(2,1)S(1)}, u32[]{:S(2)}, u32[]{:S(2)}) %collective-permute-start.1) | collective-permute-done | bytes 1048608 | tf_op jit(solution)/shard_map/ppermute | solution.py:13
  64.9 7.9 %collective-permute-start.2 = (bf16[512,1024]{1,0:T(8,128)(2,1)S(1)}, bf16[512,1024]{1,0:T(8,128)(2,1)S(1)}, u32[]{:S(2)}, u32[]{:S(2)}) collective-permute-start(bf16[512,1024]{1,0:T(8,128)(2,1)S(1)} %collective-permute-done.1), channel_id=1, source_target_pairs={{0,252},{4,0},{8,4},{12,8},{16,12},{20,16},{24,20},{28,24},{32,28}... | collective-permute-start | bytes 3145736 | tf_op jit(solution)/shard_map/ppermute | solution.py:13
  72.8 20.0 %collective-permute-done.2 = bf16[512,1024]{1,0:T(8,128)(2,1)S(1)} collective-permute-done((bf16[512,1024]{1,0:T(8,128)(2,1)S(1)}, bf16[512,1024]{1,0:T(8,128)(2,1)S(1)}, u32[]{:S(2)}, u32[]{:S(2)}) %collective-permute-start.2) | collective-permute-done | bytes 1048608 | tf_op jit(solution)/shard_map/ppermute | solution.py:13
  92.8 7.9 %collective-permute-start.3 = (bf16[512,1024]{1,0:T(8,128)(2,1)S(1)}, bf16[512,1024]{1,0:T(8,128)(2,1)S(1)}, u32[]{:S(2)}, u32[]{:S(2)}) collective-permute-start(bf16[512,1024]{1,0:T(8,128)(2,1)S(1)} %collective-permute-done.2), channel_id=1, source_target_pairs={{0,252},{4,0},{8,4},{12,8},{16,12},{20,16},{24,20},{28,24},{32,28}... | collective-permute-start | bytes 3145736 | tf_op jit(solution)/shard_map/ppermute | solution.py:13
  100.7 19.1 %collective-permute-done.3 = bf16[512,1024]{1,0:T(8,128)(2,1)S(1)} collective-permute-done((bf16[512,1024]{1,0:T(8,128)(2,1)S(1)}, bf16[512,1024]{1,0:T(8,128)(2,1)S(1)}, u32[]{:S(2)}, u32[]{:S(2)}) %collective-permute-start.3) | collective-permute-done | bytes 1048608 | tf_op jit(solution)/shard_map/ppermute | solution.py:13
  119.8 7.9 %collective-permute-start.4 = (bf16[512,1024]{1,0:T(8,128)(2,1)S(1)}, bf16[512,1024]{1,0:T(8,128)(2,1)S(1)}, u32[]{:S(2)}, u32[]{:S(2)}) collective-permute-start(bf16[512,1024]{1,0:T(8,128)(2,1)S(1)} %collective-permute-done.3), channel_id=1, source_target_pairs={{0,252},{4,0},{8,4},{12,8},{16,12},{20,16},{24,20},{28,24},{32,28}... | collective-permute-start | bytes 3145736 | tf_op jit(solution)/shard_map/ppermute | solution.py:13
  127.7 18.1 %collective-permute-done.4 = bf16[512,1024]{1,0:T(8,128)(2,1)S(1)} collective-permute-done((bf16[512,1024]{1,0:T(8,128)(2,1)S(1)}, bf16[512,1024]{1,0:T(8,128)(2,1)S(1)}, u32[]{:S(2)}, u32[]{:S(2)}) %collective-permute-start.4) | collective-permute-done | bytes 1048608 | tf_op jit(solution)/shard_map/ppermute | solution.py:13
  145.9 7.9 %collective-permute-start.5 = (bf16[512,1024]{1,0:T(8,128)(2,1)S(1)}, bf16[512,1024]{1,0:T(8,128)(2,1)S(1)}, u32[]{:S(2)}, u32[]{:S(2)}) collective-permute-start(bf16[512,1024]{1,0:T(8,128)(2,1)S(1)} %collective-permute-done.4), channel_id=1, source_target_pairs={{0,252},{4,0},{8,4},{12,8},{16,12},{20,16},{24,20},{28,24},{32,28}... | collective-permute-start | bytes 3145736 | tf_op jit(solution)/shard_map/ppermute | solution.py:13
  158.2 12.8 %collective-permute-done.5 = bf16[512,1024]{1,0:T(8,128)(2,1)S(1)} collective-permute-done((bf16[512,1024]{1,0:T(8,128)(2,1)S(1)}, bf16[512,1024]{1,0:T(8,128)(2,1)S(1)}, u32[]{:S(2)}, u32[]{:S(2)}) %collective-permute-start.5) | collective-permute-done | bytes 1048608 | tf_op jit(solution)/shard_map/ppermute | solution.py:13
  171.0 7.9 %collective-permute-start.6 = (bf16[512,1024]{1,0:T(8,128)(2,1)S(1)}, bf16[512,1024]{1,0:T(8,128)(2,1)S(1)}, u32[]{:S(2)}, u32[]{:S(2)}) collective-permute-start(bf16[512,1024]{1,0:T(8,128)(2,1)S(1)} %collective-permute-done.5), channel_id=1, source_target_pairs={{0,252},{4,0},{8,4},{12,8},{16,12},{20,16},{24,20},{28,24},{32,28}... | collective-permute-start | bytes 3145736 | tf_op jit(solution)/shard_map/ppermute | solution.py:13
  182.0 13.3 %collective-permute-done.6 = bf16[512,1024]{1,0:T(8,128)(2,1)S(1)} collective-permute-done((bf16[512,1024]{1,0:T(8,128)(2,1)S(1)}, bf16[512,1024]{1,0:T(8,128)(2,1)S(1)}, u32[]{:S(2)}, u32[]{:S(2)}) %collective-permute-start.6) | collective-permute-done | bytes 1048608 | tf_op jit(solution)/shard_map/ppermute | solution.py:13
  209.9 7.9 %collective-permute-start.9 = (f32[512,1024]{1,0:T(8,128)}, f32[512,1024]{1,0:T(8,128)}, u32[]{:S(2)}, u32[]{:S(2)}) collective-permute-start(f32[512,1024]{1,0:T(8,128)} %convolution_multiply_fusion.3), channel_id=1, source_target_pairs={{0,252},{4,0},{8,4},{12,8},{16,12},{20,16},{24,20},{28,24},{32,28}... | collective-permute-start | bytes 6291464 | tf_op jit(solution)/shard_map/ppermute | solution.py:13
  233.4 47.0 %collective-permute-done.10 = f32[512,1024]{1,0:T(8,128)} collective-permute-done((f32[512,1024]{1,0:T(8,128)S(1)}, f32[512,1024]{1,0:T(8,128)}, u32[]{:S(2)}, u32[]{:S(2)}) %collective-permute-start.10) | collective-permute-done | bytes 2097184 | tf_op jit(solution)/shard_map/ppermute | solution.py:13
  280.4 10.1 %convolution_bitcast_fusion = f32[1280,1024]{0,1:T(8,128)} fusion(bf16[512,1280]{1,0:T(8,128)(2,1)} %param.4, f32[512,1024]{1,0:T(8,128)} %fusion.4, f32[512,1024]{1,0:T(8,128)} %fusion.3, f32[512,1024]{1,0:T(8,128)} %fusion.5, f32[512,1024]{1,0:T(8,128)} %fusion.2, f32[512,1024]{1,0:T(8,128)} %fusion, f32[512,1024]{1,0:T(8,128)} %fusion.1, ...), kind=kOutput, calls=%fused_computation | convolution fusion | flops 1883766784 | bytes 21235712 | tf_op jit(solution)/shard_map/dot_general | solution.py:57
  290.6 42.0 %collective-permute-done.9 = f32[512,1024]{1,0:T(8,128)} collective-permute-done((f32[512,1024]{1,0:T(8,128)}, f32[512,1024]{1,0:T(8,128)}, u32[]{:S(2)}, u32[]{:S(2)}) %collective-permute-start.9) | collective-permute-done | bytes 2097184 | tf_op jit(solution)/shard_map/ppermute | solution.py:13
  332.5 93.2 %collective-permute-done.8 = f32[512,1024]{1,0:T(8,128)} collective-permute-done((f32[512,1024]{1,0:T(8,128)}, f32[512,1024]{1,0:T(8,128)}, u32[]{:S(2)}, u32[]{:S(2)}) %collective-permute-start.8) | collective-permute-done | bytes 2097184 | tf_op jit(solution)/shard_map/ppermute | solution.py:13
  425.8 53.3 %collective-permute-done.7 = f32[512,1024]{1,0:T(8,128)} collective-permute-done((f32[512,1024]{1,0:T(8,128)}, f32[512,1024]{1,0:T(8,128)}, u32[]{:S(2)}, u32[]{:S(2)}) %collective-permute-start.7) | collective-permute-done | bytes 2097184 | tf_op jit(solution)/shard_map/ppermute | solution.py:13
  479.1 6.8 add_convert_fusion
  485.9 237.0 %all-reduce.2.cloned.1.call-done = f32[1280,1024]{0,1:T(8,128)} async-done(((f32[1280,1024]{0,1:T(8,128)}), f32[1280,1024]{0,1:T(8,128)}) %all-reduce.2.cloned.1.call-update) | async-done | bytes 5242896 | tf_op jit(solution)/shard_map/psum | solution.py:60
  722.8 5.2 broadcast_multiply_fusion
  728.0 6.0 copy.7
  (46 shorter events, 37.6 us)
Async XLA Ops:
  7.2 146.6 %copy-start = (bf16[1280,1024]{1,0:T(8,128)(2,1)S(1)}, bf16[1280,1024]{1,0:T(8,128)(2,1)}, u32[]{:S(2)}) copy-start(bf16[1280,1024]{1,0:T(8,128)(2,1)} %param.6) | copy-start | bytes 7864324
  7.2 715.6 %all-reduce.2.cloned.1.call-start = ((), (), s32[]{:S(2)}) async-start(), calls=%async_computation | async-start | bytes 10485760 | tf_op jit(solution)/shard_map/psum | solution.py:60
  7.2 149.4 %copy-start.4 = (bf16[512,1024]{1,0:T(8,128)(2,1)S(1)}, bf16[512,1024]{1,0:T(8,128)(2,1)}, u32[]{:S(2)}) copy-start(bf16[512,1024]{1,0:T(8,128)(2,1)} %param.5) | copy-start | bytes 3145732
  7.2 33.1 %collective-permute-start = (bf16[512,1024]{1,0:T(8,128)(2,1)}, bf16[512,1024]{1,0:T(8,128)(2,1)S(1)}, u32[]{:S(2)}, u32[]{:S(2)}) collective-permute-start(bf16[512,1024]{1,0:T(8,128)(2,1)} %param.5), channel_id=1, source_target_pairs={{0,12},{4,16},{8,20},{12,24},{16,28},{20,32},{24,36},{28,40},{32,4... | collective-permute-start | bytes 3145736 | tf_op jit(solution)/shard_map/ppermute | solution.py:13
  40.4 24.5 %collective-permute-start.1 = (bf16[512,1024]{1,0:T(8,128)(2,1)S(1)}, bf16[512,1024]{1,0:T(8,128)(2,1)S(1)}, u32[]{:S(2)}, u32[]{:S(2)}) collective-permute-start(bf16[512,1024]{1,0:T(8,128)(2,1)S(1)} %collective-permute-done), channel_id=1, source_target_pairs={{0,252},{4,0},{8,4},{12,8},{16,12},{20,16},{24,20},{28,24},{32,28}... | collective-permute-start | bytes 3145736 | tf_op jit(solution)/shard_map/ppermute | solution.py:13
  64.9 27.9 %collective-permute-start.2 = (bf16[512,1024]{1,0:T(8,128)(2,1)S(1)}, bf16[512,1024]{1,0:T(8,128)(2,1)S(1)}, u32[]{:S(2)}, u32[]{:S(2)}) collective-permute-start(bf16[512,1024]{1,0:T(8,128)(2,1)S(1)} %collective-permute-done.1), channel_id=1, source_target_pairs={{0,252},{4,0},{8,4},{12,8},{16,12},{20,16},{24,20},{28,24},{32,28}... | collective-permute-start | bytes 3145736 | tf_op jit(solution)/shard_map/ppermute | solution.py:13
  92.8 27.0 %collective-permute-start.3 = (bf16[512,1024]{1,0:T(8,128)(2,1)S(1)}, bf16[512,1024]{1,0:T(8,128)(2,1)S(1)}, u32[]{:S(2)}, u32[]{:S(2)}) collective-permute-start(bf16[512,1024]{1,0:T(8,128)(2,1)S(1)} %collective-permute-done.2), channel_id=1, source_target_pairs={{0,252},{4,0},{8,4},{12,8},{16,12},{20,16},{24,20},{28,24},{32,28}... | collective-permute-start | bytes 3145736 | tf_op jit(solution)/shard_map/ppermute | solution.py:13
  119.8 26.1 %collective-permute-start.4 = (bf16[512,1024]{1,0:T(8,128)(2,1)S(1)}, bf16[512,1024]{1,0:T(8,128)(2,1)S(1)}, u32[]{:S(2)}, u32[]{:S(2)}) collective-permute-start(bf16[512,1024]{1,0:T(8,128)(2,1)S(1)} %collective-permute-done.3), channel_id=1, source_target_pairs={{0,252},{4,0},{8,4},{12,8},{16,12},{20,16},{24,20},{28,24},{32,28}... | collective-permute-start | bytes 3145736 | tf_op jit(solution)/shard_map/ppermute | solution.py:13
  145.9 25.1 %collective-permute-start.5 = (bf16[512,1024]{1,0:T(8,128)(2,1)S(1)}, bf16[512,1024]{1,0:T(8,128)(2,1)S(1)}, u32[]{:S(2)}, u32[]{:S(2)}) collective-permute-start(bf16[512,1024]{1,0:T(8,128)(2,1)S(1)} %collective-permute-done.4), channel_id=1, source_target_pairs={{0,252},{4,0},{8,4},{12,8},{16,12},{20,16},{24,20},{28,24},{32,28}... | collective-permute-start | bytes 3145736 | tf_op jit(solution)/shard_map/ppermute | solution.py:13
  156.6 51.1 %copy-start.2 = (bf16[512,1024]{1,0:T(8,128)(2,1)}, bf16[512,1024]{1,0:T(8,128)(2,1)S(1)}, u32[]{:S(2)}) copy-start(bf16[512,1024]{1,0:T(8,128)(2,1)S(1)} %convolution_convert_fusion) | copy-start | bytes 3145732
  171.0 24.2 %collective-permute-start.6 = (bf16[512,1024]{1,0:T(8,128)(2,1)S(1)}, bf16[512,1024]{1,0:T(8,128)(2,1)S(1)}, u32[]{:S(2)}, u32[]{:S(2)}) collective-permute-start(bf16[512,1024]{1,0:T(8,128)(2,1)S(1)} %collective-permute-done.5), channel_id=1, source_target_pairs={{0,252},{4,0},{8,4},{12,8},{16,12},{20,16},{24,20},{28,24},{32,28}... | collective-permute-start | bytes 3145736 | tf_op jit(solution)/shard_map/ppermute | solution.py:13
  182.0 15.0 %copy-start.6 = (s32[1,512]{1,0:T(1,128)S(1)}, s32[1,512]{1,0:T(1,128)}, u32[]{:S(2)}) copy-start(s32[1,512]{1,0:T(1,128)} %param.7) | copy-start | bytes 6148
  195.2 1.0 copy-start.5
  207.8 72.6 %collective-permute-start.10 = (f32[512,1024]{1,0:T(8,128)S(1)}, f32[512,1024]{1,0:T(8,128)}, u32[]{:S(2)}, u32[]{:S(2)}) collective-permute-start(f32[512,1024]{1,0:T(8,128)S(1)} %convolution_multiply_fusion.2), channel_id=1, source_target_pairs={{0,4},{4,8},{8,12},{12,16},{16,20},{20,24},{24,28},{28,32},{32,36}... | collective-permute-start | bytes 6291464 | tf_op jit(solution)/shard_map/ppermute | solution.py:13
  209.9 122.7 %collective-permute-start.9 = (f32[512,1024]{1,0:T(8,128)}, f32[512,1024]{1,0:T(8,128)}, u32[]{:S(2)}, u32[]{:S(2)}) collective-permute-start(f32[512,1024]{1,0:T(8,128)} %convolution_multiply_fusion.3), channel_id=1, source_target_pairs={{0,252},{4,0},{8,4},{12,8},{16,12},{20,16},{24,20},{28,24},{32,28}... | collective-permute-start | bytes 6291464 | tf_op jit(solution)/shard_map/ppermute | solution.py:13
  217.8 208.0 %collective-permute-start.8 = (f32[512,1024]{1,0:T(8,128)}, f32[512,1024]{1,0:T(8,128)}, u32[]{:S(2)}, u32[]{:S(2)}) collective-permute-start(f32[512,1024]{1,0:T(8,128)} %convolution_multiply_fusion.4), channel_id=1, source_target_pairs={{0,248},{4,252},{8,0},{12,4},{16,8},{20,12},{24,16},{28,20},{32,24... | collective-permute-start | bytes 6291464 | tf_op jit(solution)/shard_map/ppermute | solution.py:13
  219.0 260.1 %collective-permute-start.7 = (f32[512,1024]{1,0:T(8,128)}, f32[512,1024]{1,0:T(8,128)}, u32[]{:S(2)}, u32[]{:S(2)}) collective-permute-start(f32[512,1024]{1,0:T(8,128)} %convolution_multiply_fusion.5), channel_id=1, source_target_pairs={{0,244},{4,248},{8,252},{12,0},{16,4},{20,8},{24,12},{28,16},{32,2... | collective-permute-start | bytes 6291464 | tf_op jit(solution)/shard_map/ppermute | solution.py:13
  219.0 260.1 %collective-permute-start.11 = (f32[512,1024]{1,0:T(8,128)}, f32[512,1024]{1,0:T(8,128)}, u32[]{:S(2)}, u32[]{:S(2)}) collective-permute-start(f32[512,1024]{1,0:T(8,128)} %convolution_multiply_fusion.1), channel_id=1, source_target_pairs={{0,8},{4,12},{8,16},{12,20},{16,24},{20,28},{24,32},{28,36},{32,40... | collective-permute-start | bytes 6291464 | tf_op jit(solution)/shard_map/ppermute | solution.py:13
  280.4 198.7 %collective-permute-start.12 = (f32[512,1024]{1,0:T(8,128)}, f32[512,1024]{1,0:T(8,128)}, u32[]{:S(2)}, u32[]{:S(2)}) collective-permute-start(f32[512,1024]{1,0:T(8,128)} %convolution_multiply_fusion), channel_id=1, source_target_pairs={{0,12},{4,16},{8,20},{12,24},{16,28},{20,32},{24,36},{28,40},{32,4... | collective-permute-start | bytes 6291464 | tf_op jit(solution)/shard_map/ppermute | solution.py:13
  290.5 188.6 %copy-start.3 = (bf16[512,1024]{1,0:T(8,128)(2,1)S(1)}, bf16[512,1024]{1,0:T(8,128)(2,1)}, u32[]{:S(2)}) copy-start(bf16[512,1024]{1,0:T(8,128)(2,1)} %copy-done.2) | copy-start | bytes 3145732
  728.0 6.0 copy-start.1
Sparse Core Ops, SparseCore 0:
  290.7 432.0 all-reduce.1
where the time goes:
time: 742 us; the launch traced here: 741 us
  waiting for transfers between devices  606 us (82%)
  starting transfers between devices  57.6 us (8%)
  matrix products  48.8 us (7%)
  between operations  14.1 us (2%)
    ppermute x13, waiting for transfers between devices, passed_along(): lax.ppermute(shard, axis, [(i, (i + by) % length) for i in range(length)])  369 us
    psum x1, waiting for transfers between devices, on_device(): summed = lax.psum(term, ('blk', 'rep'))  237 us
    ppermute x13, starting transfers between devices, passed_along(): lax.ppermute(shard, axis, [(i, (i + by) % length) for i in range(length)])  57.5 us
    dot_general x7, matrix products, on_device(): lax.dot_general(weight, proj, (((0,), (0,)), ((), ())), preferred_element...  17.9 us
  transfers between devices with their start and end apart: 14, of which 12 were waited for; matrix products, arithmetic and copies ran while one was open for 5% of the time, Pallas kernels for 0%

commit v1 on v0

v1 whole, which is shorter than its diff:
```python
import math

import jax
import jax.numpy as jnp
from jax import lax
from jax.experimental import pallas as pl
from jax.experimental.pallas import tpu as pltpu
from jax.sharding import PartitionSpec as P

A = 1280
E = 1024
R = 512
SCALE = 4.0 / math.sqrt(E)
NX, NY, NZ = 4, 4, 8
XR = 128
TR = 128
NT = (((1,), (1,)), ((), ()))
F32 = jnp.float32
BF16 = jnp.bfloat16


def dot(a, b):
    return jnp.dot(a, b, preferred_element_type=F32)


def dot_nt(a, b):
    return lax.dot_general(a, b, NT, preferred_element_type=F32)


def part(i, size):
    return pl.ds(pl.multiple_of(i * size, size), size)


def kernel(
    aud_hbm, txt_hbm, w_hbm, pair_ref,
    loss_ref, tgrad_ref, pg_ref,
    aud, audt, w, txt, tadj, tfwd, proj, sco, wt, stat, stat_in,
    gz_out, gz_in, gs, gsum, gfwd, g_in,
    h, term, core_out, core_in, piece, in1, sum2, out2, in2, zb, zin, zall,
    loc_sem, xs, xr, ys, yr, zs, zr, ss, sr, gzs, gzr, gys, gyr,
    cs, cr, p1s, p1r, p2s, p2r, z1s, z1r, z2s, z2r, a2s, a2r, a1s, a1r, ks, kr,
):
    b = lax.axis_index("blk")
    rep = lax.axis_index("rep")
    x = lax.rem(b, NX)
    yh = lax.rem(lax.div(b, NX), 2)
    z = lax.div(b, NX * 2)
    c = lax.rem(rep, 2)
    y = yh * 2 + lax.div(rep, 2)

    def at(x_, y_, z_, c_):
        return ((z_ * 2 + lax.div(y_, 2)) * NX + x_, lax.rem(y_, 2) * 2 + c_)

    def x_peer(d):
        return at(lax.rem(x + d, NX), y, z, c)

    def y_peer(d):
        return at(x, lax.rem(y + d, NY), z, c)

    def z_peer(d):
        return at(x, y, lax.rem(z + d, NZ), c)

    sibling = at(x, y, z, 1 - c)
    step = 1 - 2 * yh
    z_next = at(x, y, lax.rem(z + step + NZ, NZ), c)
    z_back = at(x, y, lax.rem(z - step + NZ, NZ), c)

    started = []

    def send(src, dst, s, r, device):
        copy = pltpu.make_async_remote_copy(
            src_ref=src, dst_ref=dst, send_sem=s, recv_sem=r,
            device_id=device, device_id_type=pl.DeviceIdType.MESH,
        )
        copy.start()
        started.append(copy)
        return copy

    loads = [
        pltpu.make_async_copy(w_hbm, w, loc_sem.at[0]),
        pltpu.make_async_copy(aud_hbm, aud.at[0], loc_sem.at[1]),
        pltpu.make_async_copy(txt_hbm, txt, loc_sem.at[2]),
    ]
    for load in loads:
        load.start()

    barrier = pltpu.get_barrier_semaphore()
    peers = [x_peer(d) for d in range(1, NX)] + [y_peer(d) for d in range(1, NY)]
    peers += [z_peer(d) for d in range(1, NZ)] + [sibling]
    for peer in peers:
        pl.semaphore_signal(barrier, inc=1, device_id=peer, device_id_type=pl.DeviceIdType.MESH)
    pl.semaphore_wait(barrier, len(peers))

    right, left = x_peer(1), x_peer(3)
    up, down = y_peer(1), y_peer(3)
    n_x = R // XR
    rows_x = [pl.ds(i * XR, XR) for i in range(n_x)]
    rows_t = [pl.ds(i * TR, TR) for i in range(R // TR)]
    half_t = R // TR // 2
    to_right, to_left, to_up, to_down = {}, {}, {}, {}
    for i in range(n_x):
        k = n_x - 1 - i
        to_right[i] = send(aud_hbm.at[rows_x[i]], aud.at[1, rows_x[i]], xs.at[0, i], xr.at[0, i], right)
        to_left[k] = send(aud_hbm.at[rows_x[k]], aud.at[3, rows_x[k]], xs.at[1, k], xr.at[1, k], left)
        if i < half_t:
            k = half_t + i
            to_up[i] = send(txt_hbm.at[rows_t[i]], tfwd.at[rows_t[i]], ys.at[0, i], yr.at[0, i], up)
            to_down[k] = send(txt_hbm.at[rows_t[k]], tfwd.at[rows_t[k]], ys.at[0, k], yr.at[0, k], down)

    def project(d):
        @pl.loop(0, 4)
        def _(n):
            cols = part(n, 256)
            proj[d, :, cols] = dot(aud[d], w[:, cols]).astype(BF16)

    def turn(d):
        @pl.loop(0, A // 128)
        def _(n):
            cols = part(n, 128)
            audt[d, cols, :] = aud[d, :, cols].T

    def scores(index, text, d):
        @pl.loop(0, 2)
        def _(n):
            cols = part(n, 256)
            sco[index, :, cols] = SCALE * dot_nt(text[...], proj[d, cols, :])

    def row_sums(d):
        held = [d] if d == 0 else [d, 3 + d]

        def top_of(n, m):
            for k in held:
                m = jnp.maximum(m, jnp.max(sco[k, part(n, 64), :], axis=0, keepdims=True))
            return m

        m = lax.fori_loop(0, 8, top_of, jnp.full((1, R), -jnp.inf, F32))

        def total_of(n, t):
            for k in held:
                t = t + jnp.sum(jnp.exp(sco[k, part(n, 64), :] - m), axis=0, keepdims=True)
            return t

        t = lax.fori_loop(0, 8, total_of, jnp.zeros((1, R), F32))
        stat[d:d + 1, :] = m
        stat[4 + d:5 + d, :] = t

    via_z = [None] + [jnp.where(x >= d, 1 - yh, yh) for d in range(1, NX)]

    loads[0].wait()
    loads[1].wait()
    project(0)
    loads[2].wait()
    scores(0, txt, 0)
    on_up, on_down, on_z, on_right, on_left = {}, {}, {}, {}, {}
    for i in range(half_t):
        k = half_t + i
        to_up[i].wait_recv()
        on_up[i] = send(tfwd.at[rows_t[i]], tadj.at[0, rows_t[i]], ys.at[1, i], yr.at[1, i], up)
        to_down[k].wait_recv()
        on_down[k] = send(tfwd.at[rows_t[k]], tadj.at[0, rows_t[k]], ys.at[1, k], yr.at[1, k], down)
        to_right[i].wait_recv()
        on_right[i] = send(aud.at[1, rows_x[i]], aud.at[2, rows_x[i]], xs.at[0, n_x + i], xr.at[0, n_x + i], right)
        j = n_x - 1 - i
        to_left[j].wait_recv()
        on_left[j] = send(aud.at[3, rows_x[j]], aud.at[2, rows_x[j]], xs.at[1, n_x + i], xr.at[1, n_x + i], left)
    turn(0)
    row_sums(0)
    for i in range(half_t):
        k = half_t + i
        on_up[i].wait_recv()
        on_z[i] = send(tadj.at[0, rows_t[i]], tadj.at[1, rows_t[i]], zs.at[i], zr.at[i], z_next)
        on_down[k].wait_recv()
        on_z[k] = send(tadj.at[0, rows_t[k]], tadj.at[1, rows_t[k]], zs.at[k], zr.at[k], z_next)
    for i in range(n_x // 2, n_x):
        to_right[i].wait_recv()
        to_left[n_x - 1 - i].wait_recv()
    for d in (1, 3):
        project(d)
        scores(d, txt, d)
        turn(d)
    for copy in on_z.values():
        copy.wait_recv()
    for d in (1, 3):
        scores(3 + d, tadj.at[via_z[d]], d)
        row_sums(d)
    for i in range(n_x // 2):
        on_right[i].wait_recv()
        on_left[n_x - 1 - i].wait_recv()
    project(2)
    scores(2, txt, 2)
    scores(5, tadj.at[via_z[2]], 2)
    row_sums(2)

    sums = [send(stat, stat_in.at[d - 1], ss.at[d - 1], sr.at[d - 1], x_peer(d)) for d in range(1, NX)]
    turn(2)
    for copy in sums:
        copy.wait_recv()
    lse = []
    for d in range(NX):
        ms = [stat[d:d + 1, :]]
        ts = [stat[4 + d:5 + d, :]]
        for back in range(1, NX):
            k = (d - back) % NX
            ms.append(stat_in[back - 1, k:k + 1, :])
            ts.append(stat_in[back - 1, 4 + k:5 + k, :])
        top = jnp.maximum(jnp.maximum(ms[0], ms[1]), jnp.maximum(ms[2], ms[3]))
        total = sum(t * jnp.exp(m - top) for m, t in zip(ms, ts))
        lse.append(top + jnp.log(total))

    def weights(index, d):
        @pl.loop(0, 8)
        def _(n):
            rows = part(n, 64)
            wt[index, rows, :] = jnp.exp(sco[index, rows, :] - lse[d]).astype(BF16)

    for d in range(1, NX):
        weights(3 + d, d)
    zf = [None] + [v.astype(F32) for v in via_z[1:]]
    shares_z = {}
    for n in range(4):
        cols = slice(n * 256, (n + 1) * 256)
        gs_n, gz_n = None, None
        for d in range(1, NX):
            g = dot(wt[3 + d], proj[d, :, cols])
            gz_d = zf[d] * g
            gs_d = g - gz_d
            gz_n = gz_d if gz_n is None else gz_n + gz_d
            gs_n = gs_d if gs_n is None else gs_n + gs_d
        gz_out[n] = gz_n.astype(BF16)
        gs[n] = gs_n
        shares_z[n] = send(gz_out.at[n], gz_in.at[n], gzs.at[n], gzr.at[n], z_back)

    def own_weights(n, paired):
        rows = part(n, 64)
        s = sco[0, rows, :]
        column = lax.broadcasted_iota(jnp.int32, (64, R), 0) + n * 64
        hot = (pair_ref[...] == column).astype(F32)
        wt[0, rows, :] = (jnp.exp(s - lse[0]) - hot).astype(BF16)
        return paired + jnp.sum(s * hot, axis=0, keepdims=True)

    paired = lax.fori_loop(0, 8, own_weights, jnp.zeros((1, R), F32))
    loss_ref[...] = lse[0] - paired
    for d in range(1, NX):
        weights(d, d)

    @pl.loop(0, 4)
    def _(n):
        rows = part(lax.div(n, 2), 640)
        j = lax.rem(n, 2)
        texts = part(j, 256)
        own = dot_nt(audt[0, rows, :], wt[0, texts, :])
        for d in range(1, NX):
            own = own + dot_nt(audt[d, rows, :], wt[d, texts, :])
        h[rows, part(j, 256)] = own.astype(BF16)
        hs, hz = None, None
        for d in range(1, NX):
            v = dot_nt(audt[d, rows, :], wt[3 + d, texts, :])
            vz = zf[d] * v
            vs = v - vz
            hz = vz if hz is None else hz + vz
            hs = vs if hs is None else hs + vs
        h[rows, part(2 + j, 256)] = hs.astype(BF16)
        h[rows, part(4 + j, 256)] = hz.astype(BF16)

    def term_rows(which, n):
        rows = part(which, 640)
        cols = slice(n * 256, (n + 1) * 256)
        return (
            dot(h[rows, 0:512], txt[:, cols])
            + dot(h[rows, 512:1024], tadj[0, :, cols])
            + dot(h[rows, 1024:1536], tadj[1, :, cols])
        )

    pairs, firsts = {}, []

    def join(n):
        pairs[n].wait_recv()
        for p in range(8):
            rows = slice(p * 80, (p + 1) * 80)
            v = term[n, rows, :] + core_in[n, rows, :].astype(F32)
            term[n, rows, :] = v
            piece[n, p] = v.astype(BF16)
        for d in range(1, NX):
            xd, yd = lax.rem(x + d, NX), lax.rem(y + d, NY)
            firsts.append(send(piece.at[n, xd], in1.at[n, 0, d - 1], p1s.at[n, 0, d - 1], p1r.at[n, 0, d - 1], x_peer(d)))
            firsts.append(send(piece.at[n, 4 + yd], in1.at[n, 1, d - 1], p1s.at[n, 1, d - 1], p1r.at[n, 1, d - 1], y_peer(d)))

    gys_copies = {}

    def pass_share(n):
        shares_z[n].wait_recv()
        gsum[n] = (gs[n] + gz_in[n].astype(F32)).astype(BF16)
        gys_copies[n] = send(gsum.at[n], gfwd.at[n], gys.at[0, n], gyr.at[0, n], up if n < 2 else down)

    for n in range(4):
        core_out[n] = term_rows(1 - c, n).astype(BF16)
        pairs[n] = send(core_out.at[n], core_in.at[n], cs.at[n], cr.at[n], sibling)
        term[n] = term_rows(c, n)
        if n > 0:
            join(n - 1)
    join(3)
    for n in (0, 2):
        pass_share(n)

    own_grad = sco

    @pl.loop(0, 4)
    def _(n):
        cols = part(n, 256)
        g = dot(wt[0], proj[0, :, cols])
        for d in range(1, NX):
            g = g + dot(wt[d], proj[d, :, cols])
        own_grad[n, :, 0:256] = g

    for copy in firsts:
        copy.wait_recv()
    mine = (x, y)
    for n in range(4):
        for k in range(2):
            v = term[n, part(mine[k] + 4 * k, 80), :]
            for d in range(3):
                v = v + in1[n, k, d].astype(F32)
            sum2[k, n] = v
            out2[k, n] = v.astype(BF16)
    seconds = []
    for d in range(1, NX):
        xd, yd = lax.rem(x + d, NX), lax.rem(y + d, NY)
        seconds.append(send(out2.at[0, yd], in2.at[0, d - 1], p2s.at[0, d - 1], p2r.at[0, d - 1], y_peer(d)))
        seconds.append(send(out2.at[1, xd], in2.at[1, d - 1], p2s.at[1, d - 1], p2r.at[1, d - 1], x_peer(d)))
    pass_share(1)
    gys2 = {}

    def forward_share(n):
        gys_copies[n].wait_recv()
        gys2[n] = send(gfwd.at[n], g_in.at[n], gys.at[1, n], gyr.at[1, n], up if n < 2 else down)

    for copy in seconds:
        copy.wait_recv()
    theirs = (y, x)
    for k in range(2):
        v = sum2[k, theirs[k]]
        for d in range(3):
            v = v + in2[k, d].astype(F32)
        for q in range(4):
            i, j = q // 2, q % 2
            zb[4 * k + q] = v[j * 40:(j + 1) * 40, i * 128:(i + 1) * 128]
    thirds = []
    for d in range(1, NZ):
        zd = lax.rem(z + d, NZ)
        thirds.append(send(zb.at[zd], zin.at[d - 1], z1s.at[d - 1], z1r.at[d - 1], z_peer(d)))
    pass_share(3)
    forward_share(0)
    forward_share(2)
    for copy in thirds:
        copy.wait_recv()
    v = zb[z]
    for d in range(NZ - 1):
        v = v + zin[d]
    zall[z] = v * (SCALE / 256.0)
    fourths = [send(zall.at[z], zall.at[z], z2s.at[d - 1], z2r.at[d - 1], z_peer(d)) for d in range(1, NZ)]
    forward_share(1)
    for copy in fourths:
        copy.wait_recv()
    for k in range(2):
        for q in range(4):
            i, j = q // 2, q % 2
            v = zall[4 * k + q].astype(BF16)
            if k == 0:
                in2[0, 0, j * 40:(j + 1) * 40, i * 128:(i + 1) * 128] = v
            else:
                in2[1, 0, j * 40:(j + 1) * 40, i * 128:(i + 1) * 128] = v
    pg_ref[c, x, y] = in2[0, 0]
    pg_ref[c, 4 + y, x] = in2[1, 0]
    fifths = []
    for d in range(1, NX):
        fifths.append(send(pg_ref.at[c, x, y], pg_ref.at[c, x, y], a2s.at[0, d - 1], a2r.at[0, d - 1], y_peer(d)))
        fifths.append(send(pg_ref.at[c, 4 + y, x], pg_ref.at[c, 4 + y, x], a2s.at[1, d - 1], a2r.at[1, d - 1], x_peer(d)))
    forward_share(3)
    for copy in fifths:
        copy.wait_recv()
    sixths, lasts = [], []

    def to_sibling(p, k):
        lasts.append(send(pg_ref.at[c, p], pg_ref.at[c, p], ks.at[k], kr.at[k], sibling))

    for d in range(1, NX):
        sixths.append(send(pg_ref.at[c, x], pg_ref.at[c, x], a1s.at[0, d - 1], a1r.at[0, d - 1], x_peer(d)))
        sixths.append(send(pg_ref.at[c, 4 + y], pg_ref.at[c, 4 + y], a1s.at[1, d - 1], a1r.at[1, d - 1], y_peer(d)))
    to_sibling(x, 0)
    to_sibling(4 + y, 4)

    for n in range(4):
        gys2[n].wait_recv()
        cols = slice(n * 256, (n + 1) * 256)
        tgrad_ref[:, cols] = (SCALE * (own_grad[n, :, 0:256] + g_in[n].astype(F32))).astype(BF16)

    for d in range(1, NX):
        sixths[2 * (d - 1)].wait_recv()
        to_sibling(lax.rem(x + NX - d, NX), d)
        sixths[2 * (d - 1) + 1].wait_recv()
        to_sibling(4 + lax.rem(y + NY - d, NY), 4 + d)
    for copy in lasts:
        copy.wait_recv()
    for copy in started:
        copy.wait_send()


def on_device(audio_emb, text_emb, proj_weight, pair_index):
    dma = pltpu.SemaphoreType.DMA
    hbm = pl.BlockSpec(memory_space=pl.ANY)
    vmem = pl.BlockSpec(memory_space=pltpu.VMEM)
    sems = []
    for shape in ((2, R // XR + R // XR // 2), (2, R // TR), (R // TR,), (3,), (4,), (2, 4), (4,), (4, 2, 3), (2, 3), (7,), (7,), (2, 3), (2, 3), (8,)):
        sems += [dma(shape), dma(shape)]
    loss, text_grad, shares = pl.pallas_call(
        kernel,
        out_shape=(
            jax.ShapeDtypeStruct((1, R), F32),
            jax.ShapeDtypeStruct((R, E), BF16),
            jax.ShapeDtypeStruct((2, 8, 4, 80, 256), BF16),
        ),
        in_specs=[hbm, hbm, hbm, vmem],
        out_specs=(vmem, vmem, vmem),
        scratch_shapes=[
            pltpu.VMEM((4, R, A), BF16),
            pltpu.VMEM((4, A, R), BF16),
            pltpu.VMEM((A, E), BF16),
            pltpu.VMEM((R, E), BF16),
            pltpu.VMEM((2, R, E), BF16),
            pltpu.VMEM((R, E), BF16),
            pltpu.VMEM((4, R, E), BF16),
            pltpu.VMEM((7, R, R), F32),
            pltpu.VMEM((7, R, R), BF16),
            pltpu.VMEM((8, R), F32),
            pltpu.VMEM((3, 8, R), F32),
            pltpu.VMEM((4, R, 256), BF16),
            pltpu.VMEM((4, R, 256), BF16),
            pltpu.VMEM((4, R, 256), F32),
            pltpu.VMEM((4, R, 256), BF16),
            pltpu.VMEM((4, R, 256), BF16),
            pltpu.VMEM((4, R, 256), BF16),
            pltpu.VMEM((A, 3 * R), BF16),
            pltpu.VMEM((4, 640, 256), F32),
            pltpu.VMEM((4, 640, 256), BF16),
            pltpu.VMEM((4, 640, 256), BF16),
            pltpu.VMEM((4, 8, 80, 256), BF16),
            pltpu.VMEM((4, 2, 3, 80, 256), BF16),
            pltpu.VMEM((2, 4, 80, 256), F32),
            pltpu.VMEM((2, 4, 80, 256), BF16),
            pltpu.VMEM((2, 3, 80, 256), BF16),
            pltpu.VMEM((8, 40, 128), F32),
            pltpu.VMEM((7, 40, 128), F32),
            pltpu.VMEM((8, 40, 128), F32),
            dma((3,)),
            *sems,
        ],
        compiler_params=pltpu.CompilerParams(
            collective_id=0, has_side_effects=True, vmem_limit_bytes=62 * 1024 * 1024
        ),
        cost_estimate=pl.CostEstimate(flops=24 * 10**9, bytes_accessed=16 * 2**20, transcendentals=4 * 2**20),
    )(audio_emb, text_emb, proj_weight, pair_index)
    proj_grad = shares.transpose(0, 1, 3, 2, 4).reshape(A, E).astype(F32)
    return (loss.reshape(R), text_grad, proj_grad)


def solution(mesh):
    return jax.shard_map(
        on_device,
        mesh=mesh,
        in_specs=(P(("blk", "rep"), None), P(("blk", "rep"), None), P(), P(("blk", "rep"), None)),
        out_specs=(P(("blk", "rep")), P(("blk", "rep"), None), P()),
        check_vma=False,
    )
```

time: 742 us -> 142 us (0.19)
  waiting for transfers between devices: 606 us -> 0 us
  Pallas kernels: 0 us -> 130 us
  starting transfers between devices: 57.6 us -> 0 us
  matrix products: 48.8 us -> 0 us
  between operations: 14.1 us -> 0.67 us
    ppermute x13 -> x0, waiting for transfers between devices: 369 us -> none  [passed_along(): lax.ppermute(shard, axis, [(i, (i + by) % length) for i in range(length)])]
    psum x1 -> x0, waiting for transfers between devices: 237 us -> none  [on_device(): summed = lax.psum(term, ('blk', 'rep'))]
    pallas_call x0 -> x1, Pallas kernels: none -> 130 us  [on_device(): pl.pallas_call(kernel, out_shape=(jax.ShapeDtypeStruct((1, R), F32), jax....]
    ppermute x13 -> x0, starting transfers between devices: 57.5 us -> none  [passed_along(): lax.ppermute(shard, axis, [(i, (i + by) % length) for i in range(length)])]
    dot_general x22 -> x0, matrix products: 48.8 us -> none  [the longest x7 17.9 us: on_device(): lax.dot_general(weight, proj, (((0,), (0,)), ((), ())), preferred_element...]
  transfers between devices with their start and end apart: 14 -> 0, of which waited for: 12 -> 0; matrix products, arithmetic and copies ran while one was open for 5% -> 0% of each run, Pallas kernels for 0% -> 0%
where the time goes in v1:
time: 142 us
  Pallas kernels  130 us (92%)
  local copies, waits for them, and re-layouts  8.67 us (6%)
  other arithmetic  2.44 us (2%)
    pallas_call x1, Pallas kernels, on_device(): pl.pallas_call(kernel, out_shape=(jax.ShapeDtypeStruct((1, R), F32), jax....  130 us
    unnamed x7, local copies, waits for them, and re-layouts  5.21 us
    convert_element_type x1, local copies, waits for them, and re-layouts, on_device(): proj_grad = shares.transpose(0, 1, 3, 2, 4).reshape(A, E).astype(F32)  3.47 us

profile of v1, /device:TPU:1, one launch (start us, length us, event | category | flops | bytes accessed | tf_op | source)
XLA Modules:
  0.0 141.6 jit_solution(15976329007836835172)
XLA Ops:
  0.6 129.8 %shard_map.67 = (f32[1,512]{1,0:T(1,128)}, bf16[512,1024]{1,0:T(8,128)(2,1)}, bf16[2,8,4,80,256]{4,3,2,1,0:T(8,128)(2,1)}) custom-call(bf16[512,1280]{1,0:T(8,128)(2,1)} %aud_hbm.1, bf16[512,1024]{1,0:T(8,128)(2,1)} %txt_hbm.1, bf16[1280,1024]{1,0:T(8,128)(2,1)} %w_hbm.1, s32[1,512]{1,0:T(1,128)} %pair_ref.1), custom_call_target="tpu_custom_call" | custom-call | flops 24000000000 | bytes 16777216 | tf_op jit(solution)/shard_map/pallas_call | solution.py:415
  130.4 2.4 %convert_bitcast_fusion = f32[2,8,80,4,256]{4,2,3,1,0:T(8,128)S(1)} fusion(bf16[2,8,4,80,256]{4,3,2,1,0:T(8,128)(2,1)} %get-tuple-element.8), kind=kLoop, calls=%fused_computation | loop fusion | flops 1310720 | bytes 7864320 | tf_op jit(solution)/shard_map/convert_element_type | solution.py:462
  132.9 3.5 %copy.7 = f32[2,8,80,4,256]{4,3,2,1,0:T(4,128)S(1)} copy(f32[2,8,80,4,256]{4,2,3,1,0:T(8,128)S(1)} %convert_bitcast_fusion) | data formatting | bytes 10485760 | tf_op jit(solution)/shard_map/convert_element_type | solution.py:462
  136.3 0.0 copy-start.1
  136.4 0.0 copy-start
  136.4 3.6 %copy.8 = f32[160,8,4,256]{3,1,2,0:T(8,128)} copy(f32[160,8,4,256]{3,2,1,0:T(4,128)S(1)} %bitcast.6) | data formatting | bytes 10485760
  140.0 0.0 copy-done.1
  140.0 0.6 copy.11
  140.6 0.0 copy-done
  140.6 1.0 copy.12
Async XLA Ops:
  136.3 3.7 %copy-start.1 = (f32[1,512]{1,0:T(1,128)S(1)}, f32[1,512]{1,0:T(1,128)}, u32[]{:S(2)}) copy-start(f32[1,512]{1,0:T(1,128)} %get-tuple-element.6) | copy-start | bytes 6148
  136.4 4.2 %copy-start = (bf16[512,1024]{1,0:T(8,128)(2,1)S(1)}, bf16[512,1024]{1,0:T(8,128)(2,1)}, u32[]{:S(2)}) copy-start(bf16[512,1024]{1,0:T(8,128)(2,1)} %get-tuple-element.13) | copy-start | bytes 3145732

commit v2 on v0

v2 whole, which is shorter than its diff:
```python
import math

import jax
import jax.numpy as jnp
from jax import lax
from jax.experimental import pallas as pl
from jax.experimental.pallas import tpu as pltpu
from jax.sharding import PartitionSpec as P

A = 1280
E = 1024
R = 512
SCALE = 4.0 / math.sqrt(E)
NX, NY, NZ = 4, 4, 8
XR = 128
TR = 64
HALF = 256
NT = (((1,), (1,)), ((), ()))
F32 = jnp.float32
BF16 = jnp.bfloat16


def dot(a, b):
    return jnp.dot(a, b, preferred_element_type=F32)


def dot_nt(a, b):
    return lax.dot_general(a, b, NT, preferred_element_type=F32)


def part(i, size):
    return pl.ds(pl.multiple_of(i * size, size), size)


def kernel(
    aud_hbm, txt_hbm, w_hbm, pair_ref,
    loss_ref, tgrad_ref, pg_ref,
    aud, audt, w, txt, tadj, tfwd, proj, sco, wt, tops, totals, stat, stat_in,
    hacc, h, gz_in, gacc, gown, gfwd, g_in,
    core_out, core_in, piece, in1, sum2, out2, in2, zown, zb, zin, zall,
    loc_sem, xs, xr, ys, yr, zs, zr, ss, sr, gzs, gzr, gys, gyr,
    cs, cr, p1s, p1r, p2s, p2r, z1s, z1r, z2s, z2r, a2s, a2r, a1s, a1r, ks, kr,
):
    b = lax.axis_index("blk")
    rep = lax.axis_index("rep")
    x = lax.rem(b, NX)
    yh = lax.rem(lax.div(b, NX), 2)
    z = lax.div(b, NX * 2)
    c = lax.rem(rep, 2)
    y = yh * 2 + lax.div(rep, 2)

    def at(x_, y_, z_, c_):
        return ((z_ * 2 + lax.div(y_, 2)) * NX + x_, lax.rem(y_, 2) * 2 + c_)

    def x_peer(d):
        return at(lax.rem(x + d, NX), y, z, c)

    def y_peer(d):
        return at(x, lax.rem(y + d, NY), z, c)

    def z_peer(d):
        return at(x, y, lax.rem(z + d, NZ), c)

    sibling = at(x, y, z, 1 - c)
    step = 1 - 2 * yh
    z_next = at(x, y, lax.rem(z + step + NZ, NZ), c)
    z_back = at(x, y, lax.rem(z - step + NZ, NZ), c)

    started = []

    def remote(src, dst, s, r, device):
        return pltpu.make_async_remote_copy(
            src_ref=src, dst_ref=dst, send_sem=s, recv_sem=r,
            device_id=device, device_id_type=pl.DeviceIdType.MESH,
        )

    def send(src, dst, s, r, device):
        copy = remote(src, dst, s, r, device)
        copy.start()
        started.append(copy)
        return copy

    loads = [
        pltpu.make_async_copy(w_hbm, w, loc_sem.at[0]),
        pltpu.make_async_copy(aud_hbm, aud.at[0], loc_sem.at[1]),
        pltpu.make_async_copy(txt_hbm, txt, loc_sem.at[2]),
    ]
    for load in loads:
        load.start()

    barrier = pltpu.get_barrier_semaphore()
    peers = [x_peer(d) for d in range(1, NX)] + [y_peer(d) for d in range(1, NY)]
    peers += [z_peer(d) for d in range(1, NZ)] + [sibling]
    for peer in peers:
        pl.semaphore_signal(barrier, inc=1, device_id=peer, device_id_type=pl.DeviceIdType.MESH)
    pl.semaphore_wait(barrier, len(peers))

    right, left = x_peer(1), x_peer(3)
    up, down = y_peer(1), y_peer(3)
    rows_x = [pl.ds(i * XR, XR) for i in range(R // XR)]
    rows_t = [pl.ds(i * TR, TR) for i in range(R // TR)]
    n_up = R // TR // 2
    to_right, to_left, on_right, on_left = {}, {}, {}, {}
    to_up, to_down, on_up, on_down, on_z = {}, {}, {}, {}, {}

    def audio_out(half):
        i, j = 2 * half, 2 * half + 1
        for p, q in ((i, j), (j, i)):
            to_right[p] = send(aud_hbm.at[rows_x[p]], aud.at[1, rows_x[p]], xs.at[0, p], xr.at[0, p], right)
            to_left[q] = send(aud_hbm.at[rows_x[q]], aud.at[3, rows_x[q]], xs.at[1, q], xr.at[1, q], left)

    def audio_on(half):
        i, j = 2 * half, 2 * half + 1
        to_right[i].wait_recv()
        on_right[i] = send(aud.at[1, rows_x[i]], aud.at[2, rows_x[i]], xs.at[0, 4 + half], xr.at[0, 4 + half], right)
        to_left[j].wait_recv()
        on_left[j] = send(aud.at[3, rows_x[j]], aud.at[2, rows_x[j]], xs.at[1, 4 + half], xr.at[1, 4 + half], left)

    def text_out(i):
        k = n_up + i
        to_up[i] = send(txt_hbm.at[rows_t[i]], tfwd.at[rows_t[i]], ys.at[0, i], yr.at[0, i], up)
        to_down[k] = send(txt_hbm.at[rows_t[k]], tfwd.at[rows_t[k]], ys.at[0, k], yr.at[0, k], down)

    def text_on(i):
        k = n_up + i
        to_up[i].wait_recv()
        on_up[i] = send(tfwd.at[rows_t[i]], tadj.at[0, rows_t[i]], ys.at[1, i], yr.at[1, i], up)
        to_down[k].wait_recv()
        on_down[k] = send(tfwd.at[rows_t[k]], tadj.at[0, rows_t[k]], ys.at[1, k], yr.at[1, k], down)

    def text_z(i):
        k = n_up + i
        on_up[i].wait_recv()
        on_z[i] = send(tadj.at[0, rows_t[i]], tadj.at[1, rows_t[i]], zs.at[i], zr.at[i], z_next)
        on_down[k].wait_recv()
        on_z[k] = send(tadj.at[0, rows_t[k]], tadj.at[1, rows_t[k]], zs.at[k], zr.at[k], z_next)

    halves = [slice(0, HALF), slice(HALF, R)]

    def half(s):
        return part(s, HALF)

    def project(d, s):
        @pl.loop(0, 2)
        def _(n):
            cols = part(n, 512)
            proj[d, half(s), cols] = dot(aud[d, half(s), :], w[:, cols]).astype(BF16)

    def turn(d, s):
        @pl.loop(0, A // 128)
        def _(n):
            cols = part(n, 128)
            audt[d, cols, half(s)] = aud[d, half(s), cols].T

    def scores(s, index, text, d):
        @pl.loop(0, 2)
        def _(n):
            rows = pl.ds(pl.multiple_of(index * R + n * 256, 256), 256)
            sco[s, rows, :] = SCALE * dot_nt(text[part(n, 256), :], proj[d, half(s), :])

    def score_rows(index, n):
        return pl.ds(pl.multiple_of(index * R + n * 64, 64), 64)

    def exponents(s, index):
        def top_of(n, m):
            return jnp.maximum(m, jnp.max(sco[s, score_rows(index, n), :], axis=0, keepdims=True))

        m = lax.fori_loop(0, 8, top_of, jnp.full((1, HALF), -jnp.inf, F32))

        def total_of(n, t):
            e = jnp.exp(sco[s, score_rows(index, n), :] - m)
            sco[s, score_rows(index, n), :] = e
            return t + jnp.sum(e, axis=0, keepdims=True)

        tops[s, index] = m
        totals[s, index] = lax.fori_loop(0, 8, total_of, jnp.zeros((1, HALF), F32))

    def row_sums(s, d):
        m, t = tops[s, d], totals[s, d]
        if d > 0:
            m = jnp.maximum(m, tops[s, 3 + d])
            t = t * jnp.exp(tops[s, d] - m) + totals[s, 3 + d] * jnp.exp(tops[s, 3 + d] - m)
        stat[s, d:d + 1, :] = m
        stat[s, 4 + d:5 + d, :] = t

    def pair_scores(s):
        def block(n, paired):
            column = lax.broadcasted_iota(jnp.int32, (64, HALF), 0) + n * 64
            hot = (pair_ref[:, half(s)] == column).astype(F32)
            return paired + jnp.sum(sco[s, score_rows(0, n), :] * hot, axis=0, keepdims=True)

        loss_ref[:, half(s)] = lax.fori_loop(0, 8, block, jnp.zeros((1, HALF), F32))

    def sums_out(s):
        return [
            send(stat.at[s], stat_in.at[s, d - 1], ss.at[s, d - 1], sr.at[s, d - 1], x_peer(d))
            for d in range(1, NX)
        ]

    def log_sums(s):
        lse = []
        for d in range(NX):
            ms = [stat[s, d:d + 1, :]]
            ts = [stat[s, 4 + d:5 + d, :]]
            for back in range(1, NX):
                k = (d - back) % NX
                ms.append(stat_in[s, back - 1, k:k + 1, :])
                ts.append(stat_in[s, back - 1, 4 + k:5 + k, :])
            top = jnp.maximum(jnp.maximum(ms[0], ms[1]), jnp.maximum(ms[2], ms[3]))
            total = sum(t * jnp.exp(m - top) for m, t in zip(ms, ts))
            lse.append(top + jnp.log(total))
        return lse

    def weights(s, index, lse):
        factor = jnp.exp(tops[s, index] - lse)

        @pl.loop(0, 8)
        def _(n):
            wt[index, part(n, 64), :] = (sco[s, score_rows(index, n), :] * factor).astype(BF16)

    def paired_weights(s, lse):
        factor = jnp.exp(tops[s, 0] - lse)

        @pl.loop(0, 8)
        def _(n):
            column = lax.broadcasted_iota(jnp.int32, (64, HALF), 0) + n * 64
            hot = (pair_ref[:, halves[s]] == column).astype(F32)
            wt[0, part(n, 64), :] = (sco[s, score_rows(0, n), :] * factor - hot).astype(BF16)

        loss_ref[:, halves[s]] = lse - loss_ref[:, halves[s]]

    def via_z(d):
        return jnp.where(x >= d, 1 - yh, yh)

    zf = [None] + [via_z(d).astype(F32) for d in range(1, NX)]

    def adjacent_shares(s, n, cols):
        to_s, to_z = None, None
        for d in range(1, NX):
            g = dot(wt[3 + d], proj[d, halves[s], cols])
            gz = zf[d] * g
            to_z = gz if to_z is None else to_z + gz
            to_s = g - gz if to_s is None else to_s + (g - gz)
        return to_s, to_z

    def own_share(s, cols):
        g = dot(wt[0], proj[0, halves[s], cols])
        for d in range(1, NX):
            g = g + dot(wt[d], proj[d, halves[s], cols])
        return g

    def products(s):
        @pl.loop(0, 8)
        def _(n):
            rows = part(lax.div(n, 2), 320)
            j = lax.rem(n, 2)
            texts = part(j, 256)

            def keep(k, v):
                cols = part(2 * k + j, 256)
                if s == 0:
                    hacc[rows, cols] = v
                else:
                    h[rows, cols] = (hacc[rows, cols] + v).astype(BF16)

            own = dot_nt(audt[0, rows, halves[s]], wt[0, texts, :])
            for d in range(1, NX):
                own = own + dot_nt(audt[d, rows, halves[s]], wt[d, texts, :])
            keep(0, own)
            to_s, to_z = None, None
            for d in range(1, NX):
                v = dot_nt(audt[d, rows, halves[s]], wt[3 + d, texts, :])
                vz = zf[d] * v
                to_z = vz if to_z is None else to_z + vz
                to_s = v - vz if to_s is None else to_s + (v - vz)
            keep(1, to_s)
            keep(2, to_z)

    def own_scores(s, d):
        scores(s, d, txt, d)
        exponents(s, d)
        turn(d, s)

    def adjacent_scores(s, d):
        scores(s, 3 + d, tadj.at[via_z(d)], d)
        exponents(s, 3 + d)

    audio_out(0)
    text_out(0)
    text_out(1)
    loads[0].wait()
    loads[1].wait()
    loads[2].wait()

    @pl.loop(0, 2)
    def _(s):
        project(0, s)
        scores(s, 0, txt, 0)
        pair_scores(s)
        exponents(s, 0)
        turn(0, s)

    text_on(0)
    text_out(2)
    text_on(1)
    text_out(3)
    audio_on(0)
    audio_out(1)
    row_sums(0, 0)
    row_sums(1, 0)
    text_z(0)
    text_on(2)
    text_z(1)
    text_on(3)
    to_right[1].wait_recv()
    to_left[0].wait_recv()

    @pl.loop(0, 2)
    def _(n):
        project(2 * n + 1, 0)
        own_scores(0, 2 * n + 1)

    text_z(2)
    on_right[0].wait_recv()
    on_left[1].wait_recv()
    text_z(3)
    project(2, 0)
    own_scores(0, 2)
    audio_on(1)
    for copy in on_z.values():
        copy.wait_recv()

    @pl.loop(1, 4)
    def _(d):
        adjacent_scores(0, d)

    for d in range(1, NX):
        row_sums(0, d)
    sums = sums_out(0)
    to_right[3].wait_recv()
    to_left[2].wait_recv()

    @pl.loop(0, 2)
    def _(n):
        d = 2 * n + 1
        project(d, 1)
        own_scores(1, d)
        adjacent_scores(1, d)

    for copy in sums:
        copy.wait_recv()
    lse = log_sums(0)
    for d in range(1, NX):
        weights(0, 3 + d, lse[d])
        weights(0, d, lse[d])
    paired_weights(0, lse[0])

    @pl.loop(0, 4)
    def _(n):
        to_s, to_z = adjacent_shares(0, n, part(n, 256))
        gacc[0, n] = to_s
        gacc[1, n] = to_z
        gown[n] = own_share(0, part(n, 256))

    on_right[2].wait_recv()
    on_left[3].wait_recv()
    project(2, 1)
    scores(1, 2, txt, 2)
    exponents(1, 2)
    adjacent_scores(1, 2)
    for d in range(1, NX):
        row_sums(1, d)
    sums = sums_out(1)
    products(0)
    turn(2, 1)
    for copy in sums:
        copy.wait_recv()
    lse = log_sums(1)
    for d in range(1, NX):
        weights(1, 3 + d, lse[d])
    passed_on = [*on_up.values(), *on_down.values()]
    for copy in passed_on:
        copy.wait_send()
    def share_z(n):
        return remote(tfwd.at[:, part(n, 256)], gz_in.at[n], gzs.at[n], gzr.at[n], z_back)

    @pl.loop(0, 4)
    def _(n):
        to_s, to_z = adjacent_shares(1, n, part(n, 256))
        tfwd[:, part(n, 256)] = (gacc[1, n] + to_z).astype(BF16)
        gacc[0, n] = gacc[0, n] + to_s
        share_z(n).start()

    shares_z = [share_z(n) for n in range(4)]
    started.extend(shares_z)
    for d in range(1, NX):
        weights(1, d, lse[d])
    paired_weights(1, lse[0])
    products(1)

    def term_rows(which, n, i):
        rows = pl.ds(pl.multiple_of(which * 640 + i * 320, 64), 320)
        cols = part(n, 256)
        return (
            dot(h[rows, 0:512], txt[:, cols])
            + dot(h[rows, 512:1024], tadj[0, :, cols])
            + dot(h[rows, 1024:1536], tadj[1, :, cols])
        )

    def spot(n, p):
        return pl.ds(pl.multiple_of(n * 640 + p * 80, 16), 80)

    def pair_copy(n):
        return remote(core_out.at[n], core_in.at[n], cs.at[n], cr.at[n], sibling)

    def beside(k, d):
        return lax.rem((x, y)[k] + d, NX) + 4 * k

    def first_copy(n, k, d):
        return remote(
            piece.at[n, beside(k, d)], in1.at[n, k, d - 1],
            p1s.at[n, k, d - 1], p1r.at[n, k, d - 1], (x_peer, y_peer)[k](d),
        )

    first_y, second_y = {}, {}
    sides = [(pl.ds(0, HALF), up), (pl.ds(HALF, HALF), down)]

    def pass_share(n):
        shares_z[n].wait_recv()
        cols = slice(n * 256, (n + 1) * 256)
        aud[0, :, cols] = (gacc[0, n] + gz_in[n].astype(F32)).astype(BF16)
        for k, (rows, peer) in enumerate(sides):
            first_y[n, k] = send(aud.at[0, rows, cols], gfwd.at[n, rows], gys.at[0, k, n], gyr.at[0, k, n], peer)

    def forward_share(n):
        for k, (rows, peer) in enumerate(sides):
            first_y[n, k].wait_recv()
            second_y[n, k] = send(gfwd.at[n, rows], g_in.at[n, rows], gys.at[1, k, n], gyr.at[1, k, n], peer)

    @pl.loop(0, 5)
    def _(n):
        @pl.when(n < 4)
        def _():
            @pl.loop(0, 2)
            def _(i):
                core_out[n, part(i, 320), :] = term_rows(1 - c, n, i).astype(BF16)

            pair_copy(n).start()

            @pl.loop(0, 2)
            def _(i):
                sco[0, pl.ds(pl.multiple_of(n * 640 + i * 320, 64), 320), :] = term_rows(c, n, i)

        @pl.when(n > 0)
        def _():
            pair_copy(n - 1).wait_recv()

            @pl.loop(0, 8)
            def _(p):
                v = sco[0, spot(n - 1, p), :] + core_in[n - 1, pl.ds(pl.multiple_of(p * 80, 16), 80), :].astype(F32)
                sco[0, spot(n - 1, p), :] = v
                piece[n - 1, p] = v.astype(BF16)

            for d in range(1, NX):
                for k in range(2):
                    first_copy(n - 1, k, d).start()

    firsts = [first_copy(n, k, d) for n in range(4) for k in range(2) for d in range(1, NX)]
    started.extend(firsts)
    started.extend(pair_copy(n) for n in range(4))
    pass_share(0)

    @pl.loop(0, 4)
    def _(n):
        gown[n] = gown[n] + own_share(1, part(n, 256))

    for copy in firsts:
        copy.wait_recv()
    mine = (x, 4 + y)
    for n in range(4):
        for k in range(2):
            v = sco[0, spot(n, mine[k]), :]
            for d in range(3):
                v = v + in1[n, k, d].astype(F32)
            sum2[k, n] = v
            out2[k, n] = v.astype(BF16)
    seconds = []
    for d in range(1, NX):
        xd, yd = lax.rem(x + d, NX), lax.rem(y + d, NY)
        seconds.append(send(out2.at[0, yd], in2.at[0, d - 1], p2s.at[0, d - 1], p2r.at[0, d - 1], y_peer(d)))
        seconds.append(send(out2.at[1, xd], in2.at[1, d - 1], p2s.at[1, d - 1], p2r.at[1, d - 1], x_peer(d)))
    pass_share(1)

    for copy in seconds:
        copy.wait_recv()
    theirs = (y, x)
    tiles = [(k, i, j) for k in range(2) for i in range(5) for j in range(2)]
    for k in range(2):
        v = sum2[k, theirs[k]]
        for d in range(3):
            v = v + in2[k, d].astype(F32)
        for t, (k_, i, j) in enumerate(tiles):
            if k_ == k:
                tile = v[i * 16:(i + 1) * 16, j * 128:(j + 1) * 128]
                zown[t // 3, t % 3] = tile
                zb[t // 3, t % 3] = tile.astype(BF16)
    for t in range(20, 24):
        zown[t // 3, t % 3] = jnp.zeros((16, 128), F32)
        zb[t // 3, t % 3] = jnp.zeros((16, 128), BF16)
    thirds = []
    for d in range(1, NZ):
        zd = lax.rem(z + d, NZ)
        thirds.append(send(zb.at[zd], zin.at[d - 1], z1s.at[d - 1], z1r.at[d - 1], z_peer(d)))
    forward_share(0)
    pass_share(2)
    for copy in thirds:
        copy.wait_recv()
    v = zown[z]
    for d in range(NZ - 1):
        v = v + zin[d].astype(F32)
    zall[z] = (v * (SCALE / 256.0)).astype(BF16)
    fourths = [send(zall.at[z], zall.at[z], z2s.at[d - 1], z2r.at[d - 1], z_peer(d)) for d in range(1, NZ)]
    forward_share(1)
    for copy in fourths:
        copy.wait_recv()

    def block(p, rows=80, more=0):
        return pl.ds(pl.multiple_of(c * 640 + p * 80 + more, 16), rows)

    def columns(n, size=256, more=0):
        return pl.ds(pl.multiple_of(n * 256 + more, 128), size)

    for t, (k, i, j) in enumerate(tiles):
        pg_ref[block(mine[k], 16, 16 * i), columns(theirs[k], 128, 128 * j)] = zall[t // 3, t % 3]
    fifths = []
    for k in range(2):
        own = pg_ref.at[block(mine[k]), columns(theirs[k])]
        for d in range(1, NX):
            fifths.append(send(own, own, a2s.at[k, d - 1], a2r.at[k, d - 1], (y_peer, x_peer)[k](d)))
    pass_share(3)
    forward_share(2)
    for copy in fifths:
        copy.wait_recv()
    sixths, lasts = {}, []

    def to_sibling(p, k):
        rows = pg_ref.at[block(p)]
        lasts.append(send(rows, rows, ks.at[k], kr.at[k], sibling))

    low, high = pl.ds(0, 512), pl.ds(512, 512)

    def spread(k, i, p, cols, peer):
        rows = pg_ref.at[block(p), cols]
        sixths[k, i] = send(rows, rows, a1s.at[k, i], a1r.at[k, i], peer)

    ends = [(x_peer(1), x_peer(3)), (y_peer(1), y_peer(3))]
    for k in range(2):
        spread(k, 0, mine[k], low, ends[k][0])
        spread(k, 1, mine[k], high, ends[k][1])
    for k in range(2):
        spread(k, 2, mine[k], high, ends[k][0])
        spread(k, 3, mine[k], low, ends[k][1])
        to_sibling(mine[k], 4 * k)
    for k in range(2):
        sixths[k, 0].wait_recv()
        spread(k, 4, beside(k, 3), low, ends[k][0])
        sixths[k, 1].wait_recv()
        spread(k, 5, beside(k, 1), high, ends[k][1])
    forward_share(3)

    for n in range(4):
        for k in range(2):
            second_y[n, k].wait_recv()
        tgrad_ref[:, n * 256:(n + 1) * 256] = (SCALE * (gown[n] + g_in[n].astype(F32))).astype(BF16)

    for d, i, j in ((3, 0, 2), (1, 1, 3), (2, 4, 5)):
        for k in range(2):
            if d == 2:
                sixths[k, i].wait_recv()
            sixths[k, j].wait_recv()
            to_sibling(beside(k, d), 4 * k + d)
    for copy in lasts:
        copy.wait_recv()
    for copy in started:
        if not any(copy is other for other in passed_on):
            copy.wait_send()


def finish(loss_in, text_in, proj_in, loss_ref, text_ref, proj_ref):
    loss_ref[...] = loss_in[0, :]
    text_ref[...] = text_in[...]
    proj_ref[...] = proj_in[...].astype(F32)


def on_device(audio_emb, text_emb, proj_weight, pair_index):
    dma = pltpu.SemaphoreType.DMA
    hbm = pl.BlockSpec(memory_space=pl.ANY)
    vmem = pl.BlockSpec(memory_space=pltpu.VMEM)
    sems = []
    for shape in ((2, 6), (2, R // TR), (R // TR,), (2, 3), (4,), (2, 2, 4), (4,), (4, 2, 3), (2, 3), (7,), (7,), (2, 3), (2, 6), (8,)):
        sems += [dma(shape), dma(shape)]
    loss, text_grad, shares = pl.pallas_call(
        kernel,
        out_shape=(
            jax.ShapeDtypeStruct((1, R), F32),
            jax.ShapeDtypeStruct((R, E), BF16),
            jax.ShapeDtypeStruct((A, E), BF16),
        ),
        in_specs=[hbm, hbm, hbm, vmem],
        out_specs=(vmem, vmem, vmem),
        scratch_shapes=[
            pltpu.VMEM((4, R, A), BF16),
            pltpu.VMEM((4, A, R), BF16),
            pltpu.VMEM((A, E), BF16),
            pltpu.VMEM((R, E), BF16),
            pltpu.VMEM((2, R, E), BF16),
            pltpu.VMEM((R, E), BF16),
            pltpu.VMEM((4, R, E), BF16),
            pltpu.VMEM((2, 7 * R, HALF), F32),
            pltpu.VMEM((7, R, HALF), BF16),
            pltpu.VMEM((2, 7, 1, HALF), F32),
            pltpu.VMEM((2, 7, 1, HALF), F32),
            pltpu.VMEM((2, 8, HALF), F32),
            pltpu.VMEM((2, 3, 8, HALF), F32),
            pltpu.VMEM((A, 3 * R), F32),
            pltpu.VMEM((A, 3 * R), BF16),
            pltpu.VMEM((4, R, 256), BF16),
            pltpu.VMEM((2, 4, R, 256), F32),
            pltpu.VMEM((4, R, 256), F32),
            pltpu.VMEM((4, R, 256), BF16),
            pltpu.VMEM((4, R, 256), BF16),
            pltpu.VMEM((4, 640, 256), BF16),
            pltpu.VMEM((4, 640, 256), BF16),
            pltpu.VMEM((4, 8, 80, 256), BF16),
            pltpu.VMEM((4, 2, 3, 80, 256), BF16),
            pltpu.VMEM((2, 4, 80, 256), F32),
            pltpu.VMEM((2, 4, 80, 256), BF16),
            pltpu.VMEM((2, 3, 80, 256), BF16),
            pltpu.VMEM((8, 3, 16, 128), F32),
            pltpu.VMEM((8, 3, 16, 128), BF16),
            pltpu.VMEM((7, 3, 16, 128), BF16),
            pltpu.VMEM((8, 3, 16, 128), BF16),
            dma((3,)),
            *sems,
        ],
        compiler_params=pltpu.CompilerParams(
            collective_id=0, has_side_effects=True, vmem_limit_bytes=63 * 1024 * 1024
        ),
        cost_estimate=pl.CostEstimate(flops=24 * 10**9, bytes_accessed=16 * 2**20, transcendentals=4 * 2**20),
    )(audio_emb, text_emb, proj_weight, pair_index)
    return pl.pallas_call(
        finish,
        grid=(4,),
        out_shape=(
            jax.ShapeDtypeStruct((R,), F32),
            jax.ShapeDtypeStruct((R, E), BF16),
            jax.ShapeDtypeStruct((A, E), F32),
        ),
        in_specs=[
            pl.BlockSpec((1, R), lambda i: (0, 0)),
            pl.BlockSpec((R // 4, E), lambda i: (i, 0)),
            pl.BlockSpec((A // 4, E), lambda i: (i, 0)),
        ],
        out_specs=(
            pl.BlockSpec((R,), lambda i: (0,)),
            pl.BlockSpec((R // 4, E), lambda i: (i, 0)),
            pl.BlockSpec((A // 4, E), lambda i: (i, 0)),
        ),
        cost_estimate=pl.CostEstimate(flops=0, bytes_accessed=10 * 2**20, transcendentals=0),
    )(loss, text_grad, shares)


def solution(mesh):
    return jax.shard_map(
        on_device,
        mesh=mesh,
        in_specs=(P(("blk", "rep"), None), P(("blk", "rep"), None), P(), P(("blk", "rep"), None)),
        out_specs=(P(("blk", "rep")), P(("blk", "rep"), None), P()),
        check_vma=False,
    )
```

time: 742 us -> 136 us (0.18)
  waiting for transfers between devices: 606 us -> 0 us
  Pallas kernels: 0 us -> 136 us
  starting transfers between devices: 57.6 us -> 0 us
  matrix products: 48.8 us -> 0 us
  between operations: 14.1 us -> 0.64 us
    ppermute x13 -> x0, waiting for transfers between devices: 369 us -> none  [passed_along(): lax.ppermute(shard, axis, [(i, (i + by) % length) for i in range(length)])]
    psum x1 -> x0, waiting for transfers between devices: 237 us -> none  [on_device(): summed = lax.psum(term, ('blk', 'rep'))]
    pallas_call x0 -> x2, Pallas kernels: none -> 136 us  [the longest x1 130 us: on_device(): pl.pallas_call(kernel, out_shape=(jax.ShapeDtypeStruct((1, R), F32), jax....]
    ppermute x13 -> x0, starting transfers between devices: 57.5 us -> none  [passed_along(): lax.ppermute(shard, axis, [(i, (i + by) % length) for i in range(length)])]
    dot_general x22 -> x0, matrix products: 48.8 us -> none  [the longest x7 17.9 us: on_device(): lax.dot_general(weight, proj, (((0,), (0,)), ((), ())), preferred_element...]
  transfers between devices with their start and end apart: 14 -> 0, of which waited for: 12 -> 0; matrix products, arithmetic and copies ran while one was open for 5% -> 0% of each run, Pallas kernels for 0% -> 0%
where the time goes in v2:
time: 136 us
  Pallas kernels  136 us (100%)
    pallas_call x1, Pallas kernels, on_device(): pl.pallas_call(kernel, out_shape=(jax.ShapeDtypeStruct((1, R), F32), jax....  130 us
    pallas_call x1, Pallas kernels, on_device(): pl.pallas_call(finish, grid=(4,), out_shape=(jax.ShapeDtypeStruct((R,), F...  5.13 us

profile of v2, /device:TPU:1, one launch (start us, length us, event | category | flops | bytes accessed | tf_op | source)
XLA Modules:
  0.0 136.2 jit_solution(194290449757795494)
XLA Ops:
  0.6 130.5 %shard_map.67 = (f32[1,512]{1,0:T(1,128)}, bf16[512,1024]{1,0:T(8,128)(2,1)}, bf16[1280,1024]{1,0:T(8,128)(2,1)}) custom-call(bf16[512,1280]{1,0:T(8,128)(2,1)} %aud_hbm.1, bf16[512,1024]{1,0:T(8,128)(2,1)} %txt_hbm.1, bf16[1280,1024]{1,0:T(8,128)(2,1)} %w_hbm.1, s32[1,512]{1,0:T(1,128)} %pair_ref.1), custom_call_target="tpu_custom_call" | custom-call | flops 24000000000 | bytes 16777216 | tf_op jit(solution)/shard_map/pallas_call | solution.py:602
  131.1 5.1 %shard_map.68 = (f32[512]{0:T(512)}, bf16[512,1024]{1,0:T(8,128)(2,1)}, f32[1280,1024]{1,0:T(8,128)}) custom-call(f32[1,512]{1,0:T(1,128)} %get-tuple-element.6.loss_in, bf16[512,1024]{1,0:T(8,128)(2,1)} %get-tuple-element.7.text_in, bf16[1280,1024]{1,0:T(8,128)(2,1)} %get-tuple-element.8.proj_in), custom_call_target="tpu_custom_call" | custom-call | bytes 10485760 | tf_op jit(solution)/shard_map/pallas_call | solution.py:651

commit v3 on v2

--- a/solution.py
+++ b/solution.py
@@ -34,11 +34,11 @@
 
 def kernel(
     aud_hbm, txt_hbm, w_hbm, pair_ref,
-    loss_ref, tgrad_ref, pg_ref,
-    aud, audt, w, txt, tadj, tfwd, proj, sco, wt, tops, totals, stat, stat_in,
-    hacc, h, gz_in, gacc, gown, gfwd, g_in,
+    loss_ref, tgrad_out, pg_out,
+    aud, audt, w, txt, tadj, tfwd, tz, proj, sco, wt, wo, tops, totals, stat, stat_in,
+    tgrad_ref, pg_ref, hacc, h, gz_in, gacc, gfwd, g_in,
     core_out, core_in, piece, in1, sum2, out2, in2, zown, zb, zin, zall,
-    loc_sem, xs, xr, ys, yr, zs, zr, ss, sr, gzs, gzr, gys, gyr,
+    loc_sem, out_sem, xs, xr, ys, yr, es, er, zs, zr, ss, sr, gzs, gzr, gys, gyr,
     cs, cr, p1s, p1r, p2s, p2r, z1s, z1r, z2s, z2r, a2s, a2r, a1s, a1r, ks, kr,
 ):
     b = lax.axis_index("blk")
@@ -134,6 +134,24 @@
         on_z[i] = send(tadj.at[0, rows_t[i]], tadj.at[1, rows_t[i]], zs.at[i], zr.at[i], z_next)
         on_down[k].wait_recv()
         on_z[k] = send(tadj.at[0, rows_t[k]], tadj.at[1, rows_t[k]], zs.at[k], zr.at[k], z_next)
+
+    z_up, z_down = n_up - 1, 2 * n_up - 1
+    ways = [(z_up, up), (z_down, down)]
+    early, early_on, early_last = {}, {}, {}
+
+    def early_out():
+        for k, (i, _) in enumerate(ways):
+            early[k] = send(txt_hbm.at[rows_t[i]], tz.at[0, k], es.at[0, k], er.at[0, k], z_back)
+
+    def early_y():
+        for k, (i, peer) in enumerate(ways):
+            early[k].wait_recv()
+            early_on[k] = send(tz.at[0, k], tz.at[1, k], es.at[1, k], er.at[1, k], peer)
+
+    def early_end():
+        for k, (i, peer) in enumerate(ways):
+            early_on[k].wait_recv()
+            early_last[k] = send(tz.at[1, k], tadj.at[1, rows_t[i]], es.at[2, k], er.at[2, k], peer)
 
     halves = [slice(0, HALF), slice(HALF, R)]
 
@@ -213,10 +231,11 @@
 
     def weights(s, index, lse):
         factor = jnp.exp(tops[s, index] - lse)
+        place = wt.at[index - 4] if index > 3 else wo.at[s, index]
 
         @pl.loop(0, 8)
         def _(n):
-            wt[index, part(n, 64), :] = (sco[s, score_rows(index, n), :] * factor).astype(BF16)
+            place[part(n, 64), :] = (sco[s, score_rows(index, n), :] * factor).astype(BF16)
 
     def paired_weights(s, lse):
         factor = jnp.exp(tops[s, 0] - lse)
@@ -225,7 +244,7 @@
         def _(n):
             column = lax.broadcasted_iota(jnp.int32, (64, HALF), 0) + n * 64
             hot = (pair_ref[:, halves[s]] == column).astype(F32)
-            wt[0, part(n, 64), :] = (sco[s, score_rows(0, n), :] * factor - hot).astype(BF16)
+            wo[s, 0, part(n, 64), :] = (sco[s, score_rows(0, n), :] * factor - hot).astype(BF16)
 
         loss_ref[:, halves[s]] = lse - loss_ref[:, halves[s]]
 
@@ -237,22 +256,24 @@
     def adjacent_shares(s, n, cols):
         to_s, to_z = None, None
         for d in range(1, NX):
-            g = dot(wt[3 + d], proj[d, halves[s], cols])
+            g = dot(wt[d - 1], proj[d, halves[s], cols])
             gz = zf[d] * g
             to_z = gz if to_z is None else to_z + gz
             to_s = g - gz if to_s is None else to_s + (g - gz)
         return to_s, to_z
 
-    def own_share(s, cols):
-        g = dot(wt[0], proj[0, halves[s], cols])
-        for d in range(1, NX):
-            g = g + dot(wt[d], proj[d, halves[s], cols])
+    def own_share(cols):
+        g = None
+        for s in range(2):
+            for d in range(NX):
+                v = dot(wo[s, d], proj[d, halves[s], cols])
+                g = v if g is None else g + v
         return g
 
     def products(s):
-        @pl.loop(0, 8)
+        @pl.loop(0, 4)
         def _(n):
-            rows = part(lax.div(n, 2), 320)
+            rows = part(lax.div(n, 2), 640)
             j = lax.rem(n, 2)
             texts = part(j, 256)
 
@@ -263,13 +284,13 @@
                 else:
                     h[rows, cols] = (hacc[rows, cols] + v).astype(BF16)
 
-            own = dot_nt(audt[0, rows, halves[s]], wt[0, texts, :])
+            own = dot_nt(audt[0, rows, halves[s]], wo[s, 0, texts, :])
             for d in range(1, NX):
-                own = own + dot_nt(audt[d, rows, halves[s]], wt[d, texts, :])
+                own = own + dot_nt(audt[d, rows, halves[s]], wo[s, d, texts, :])
             keep(0, own)
             to_s, to_z = None, None
             for d in range(1, NX):
-                v = dot_nt(audt[d, rows, halves[s]], wt[3 + d, texts, :])
+                v = dot_nt(audt[d, rows, halves[s]], wt[d - 1, texts, :])
                 vz = zf[d] * v
                 to_z = vz if to_z is None else to_z + vz
                 to_s = v - vz if to_s is None else to_s + (v - vz)
@@ -287,6 +308,7 @@
 
     audio_out(0)
     text_out(0)
+    early_out()
     text_out(1)
     loads[0].wait()
     loads[1].wait()
@@ -303,6 +325,7 @@
     text_on(0)
     text_out(2)
     text_on(1)
+    early_y()
     text_out(3)
     audio_on(0)
     audio_out(1)
@@ -311,6 +334,7 @@
     text_z(0)
     text_on(2)
     text_z(1)
+    early_end()
     text_on(3)
     to_right[1].wait_recv()
     to_left[0].wait_recv()
@@ -323,11 +347,10 @@
     text_z(2)
     on_right[0].wait_recv()
     on_left[1].wait_recv()
-    text_z(3)
     project(2, 0)
     own_scores(0, 2)
     audio_on(1)
-    for copy in on_z.values():
+    for copy in [*on_z.values(), *early_last.values(), on_up[n_up - 1], on_down[2 * n_up - 1]]:
         copy.wait_recv()
 
     @pl.loop(1, 4)
@@ -360,7 +383,6 @@
         to_s, to_z = adjacent_shares(0, n, part(n, 256))
         gacc[0, n] = to_s
         gacc[1, n] = to_z
-        gown[n] = own_share(0, part(n, 256))
 
     on_right[2].wait_recv()
     on_left[3].wait_recv()
@@ -398,8 +420,8 @@
     paired_weights(1, lse[0])
     products(1)
 
-    def term_rows(which, n, i):
-        rows = pl.ds(pl.multiple_of(which * 640 + i * 320, 64), 320)
+    def term_rows(which, n):
+        rows = part(which, 640)
         cols = part(n, 256)
         return (
             dot(h[rows, 0:512], txt[:, cols])
@@ -441,15 +463,9 @@
     def _(n):
         @pl.when(n < 4)
         def _():
-            @pl.loop(0, 2)
-            def _(i):
-                core_out[n, part(i, 320), :] = term_rows(1 - c, n, i).astype(BF16)
-
+            core_out[n] = term_rows(1 - c, n).astype(BF16)
             pair_copy(n).start()
-
-            @pl.loop(0, 2)
-            def _(i):
-                sco[0, pl.ds(pl.multiple_of(n * 640 + i * 320, 64), 320), :] = term_rows(c, n, i)
+            sco[0, part(n, 640), :] = term_rows(c, n)
 
         @pl.when(n > 0)
         def _():
@@ -461,7 +477,7 @@
                 sco[0, spot(n - 1, p), :] = v
                 piece[n - 1, p] = v.astype(BF16)
 
-            for d in range(1, NX):
+            for d in (2, 1, 3):
                 for k in range(2):
                     first_copy(n - 1, k, d).start()
 
@@ -470,10 +486,13 @@
     started.extend(pair_copy(n) for n in range(4))
     pass_share(0)
 
-    @pl.loop(0, 4)
-    def _(n):
-        gown[n] = gown[n] + own_share(1, part(n, 256))
-
+    def own_gradient(first, last):
+        @pl.loop(first, last)
+        def _(n):
+            cols = part(n, 256)
+            hacc[0:R, cols] = own_share(cols)
+
+    own_gradient(0, 2)
     for copy in firsts:
         copy.wait_recv()
     mine = (x, 4 + y)
@@ -485,12 +504,12 @@
             sum2[k, n] = v
             out2[k, n] = v.astype(BF16)
     seconds = []
-    for d in range(1, NX):
+    for d in (2, 1, 3):
         xd, yd = lax.rem(x + d, NX), lax.rem(y + d, NY)
         seconds.append(send(out2.at[0, yd], in2.at[0, d - 1], p2s.at[0, d - 1], p2r.at[0, d - 1], y_peer(d)))
         seconds.append(send(out2.at[1, xd], in2.at[1, d - 1], p2s.at[1, d - 1], p2r.at[1, d - 1], x_peer(d)))
     pass_share(1)
-
+    own_gradient(2, 4)
     for copy in seconds:
         copy.wait_recv()
     theirs = (y, x)
@@ -508,7 +527,8 @@
         zown[t // 3, t % 3] = jnp.zeros((16, 128), F32)
         zb[t // 3, t % 3] = jnp.zeros((16, 128), BF16)
     thirds = []
-    for d in range(1, NZ):
+    far_first = (4, 3, 5, 2, 6, 1, 7)
+    for d in far_first:
         zd = lax.rem(z + d, NZ)
         thirds.append(send(zb.at[zd], zin.at[d - 1], z1s.at[d - 1], z1r.at[d - 1], z_peer(d)))
     forward_share(0)
@@ -519,7 +539,7 @@
     for d in range(NZ - 1):
         v = v + zin[d].astype(F32)
     zall[z] = (v * (SCALE / 256.0)).astype(BF16)
-    fourths = [send(zall.at[z], zall.at[z], z2s.at[d - 1], z2r.at[d - 1], z_peer(d)) for d in range(1, NZ)]
+    fourths = [send(zall.at[z], zall.at[z], z2s.at[d - 1], z2r.at[d - 1], z_peer(d)) for d in far_first]
     forward_share(1)
     for copy in fourths:
         copy.wait_recv()
@@ -535,16 +555,23 @@
     fifths = []
     for k in range(2):
         own = pg_ref.at[block(mine[k]), columns(theirs[k])]
-        for d in range(1, NX):
+        for d in (2, 1, 3):
             fifths.append(send(own, own, a2s.at[k, d - 1], a2r.at[k, d - 1], (y_peer, x_peer)[k](d)))
     pass_share(3)
     forward_share(2)
     for copy in fifths:
         copy.wait_recv()
-    sixths, lasts = {}, []
+    sixths, lasts, written, blocks = {}, [], [], []
+
+    def write(src, dst, k):
+        copy = pltpu.make_async_copy(src, dst, out_sem.at[k])
+        copy.start()
+        written.append(copy)
 
     def to_sibling(p, k):
         rows = pg_ref.at[block(p)]
+        write(rows, pg_out.at[block(p)], k)
+        blocks.append((p, k))
         lasts.append(send(rows, rows, ks.at[k], kr.at[k], sibling))
 
     low, high = pl.ds(0, 512), pl.ds(512, 512)
@@ -571,7 +598,8 @@
     for n in range(4):
         for k in range(2):
             second_y[n, k].wait_recv()
-        tgrad_ref[:, n * 256:(n + 1) * 256] = (SCALE * (gown[n] + g_in[n].astype(F32))).astype(BF16)
+        tgrad_ref[:, n * 256:(n + 1) * 256] = (SCALE * (hacc[0:R, n * 256:(n + 1) * 256] + g_in[n].astype(F32))).astype(BF16)
+    write(tgrad_ref, tgrad_out, 16)
 
     for d, i, j in ((3, 0, 2), (1, 1, 3), (2, 4, 5)):
         for k in range(2):
@@ -579,8 +607,12 @@
                 sixths[k, i].wait_recv()
             sixths[k, j].wait_recv()
             to_sibling(beside(k, d), 4 * k + d)
-    for copy in lasts:
-        copy.wait_recv()
+    for copy, (p, k) in zip(lasts, blocks):
+        copy.wait_recv()
+        rows = pl.ds(pl.multiple_of((1 - c) * 640 + p * 80, 16), 80)
+        write(pg_ref.at[rows], pg_out.at[rows], 8 + k)
+    for copy in written:
+        copy.wait()
     for copy in started:
         if not any(copy is other for other in passed_on):
             copy.wait_send()
@@ -597,7 +629,7 @@
     hbm = pl.BlockSpec(memory_space=pl.ANY)
     vmem = pl.BlockSpec(memory_space=pltpu.VMEM)
     sems = []
-    for shape in ((2, 6), (2, R // TR), (R // TR,), (2, 3), (4,), (2, 2, 4), (4,), (4, 2, 3), (2, 3), (7,), (7,), (2, 3), (2, 6), (8,)):
+    for shape in ((2, 6), (2, R // TR), (3, 2), (R // TR,), (2, 3), (4,), (2, 2, 4), (4,), (4, 2, 3), (2, 3), (7,), (7,), (2, 3), (2, 6), (8,)):
         sems += [dma(shape), dma(shape)]
     loss, text_grad, shares = pl.pallas_call(
         kernel,
@@ -607,7 +639,7 @@
             jax.ShapeDtypeStruct((A, E), BF16),
         ),
         in_specs=[hbm, hbm, hbm, vmem],
-        out_specs=(vmem, vmem, vmem),
+        out_specs=(vmem, hbm, hbm),
         scratch_shapes=[
             pltpu.VMEM((4, R, A), BF16),
             pltpu.VMEM((4, A, R), BF16),
@@ -615,18 +647,21 @@
             pltpu.VMEM((R, E), BF16),
             pltpu.VMEM((2, R, E), BF16),
             pltpu.VMEM((R, E), BF16),
+            pltpu.VMEM((2, 2, TR, E), BF16),
             pltpu.VMEM((4, R, E), BF16),
             pltpu.VMEM((2, 7 * R, HALF), F32),
-            pltpu.VMEM((7, R, HALF), BF16),
+            pltpu.VMEM((3, R, HALF), BF16),
+            pltpu.VMEM((2, 4, R, HALF), BF16),
             pltpu.VMEM((2, 7, 1, HALF), F32),
             pltpu.VMEM((2, 7, 1, HALF), F32),
             pltpu.VMEM((2, 8, HALF), F32),
             pltpu.VMEM((2, 3, 8, HALF), F32),
+            pltpu.VMEM((R, E), BF16),
+            pltpu.VMEM((A, E), BF16),
             pltpu.VMEM((A, 3 * R), F32),
             pltpu.VMEM((A, 3 * R), BF16),
             pltpu.VMEM((4, R, 256), BF16),
             pltpu.VMEM((2, 4, R, 256), F32),
-            pltpu.VMEM((4, R, 256), F32),
             pltpu.VMEM((4, R, 256), BF16),
             pltpu.VMEM((4, R, 256), BF16),
             pltpu.VMEM((4, 640, 256), BF16),
@@ -641,6 +676,7 @@
             pltpu.VMEM((7, 3, 16, 128), BF16),
             pltpu.VMEM((8, 3, 16, 128), BF16),
             dma((3,)),
+            dma((17,)),
             *sems,
         ],
         compiler_params=pltpu.CompilerParams(
@@ -650,7 +686,7 @@
     )(audio_emb, text_emb, proj_weight, pair_index)
     return pl.pallas_call(
         finish,
-        grid=(4,),
+        grid=(2,),
         out_shape=(
             jax.ShapeDtypeStruct((R,), F32),
             jax.ShapeDtypeStruct((R, E), BF16),
@@ -658,13 +694,13 @@
         ),
         in_specs=[
             pl.BlockSpec((1, R), lambda i: (0, 0)),
-            pl.BlockSpec((R // 4, E), lambda i: (i, 0)),
-            pl.BlockSpec((A // 4, E), lambda i: (i, 0)),
+            pl.BlockSpec((R // 2, E), lambda i: (i, 0)),
+            pl.BlockSpec((A // 2, E), lambda i: (i, 0)),
         ],
         out_specs=(
             pl.BlockSpec((R,), lambda i: (0,)),
-            pl.BlockSpec((R // 4, E), lambda i: (i, 0)),
-            pl.BlockSpec((A // 4, E), lambda i: (i, 0)),
+            pl.BlockSpec((R // 2, E), lambda i: (i, 0)),
+            pl.BlockSpec((A // 2, E), lambda i: (i, 0)),
         ),
         cost_estimate=pl.CostEstimate(flops=0, bytes_accessed=10 * 2**20, transcendentals=0),
     )(loss, text_grad, shares)

time: 136 us -> 133 us (0.978)
  Pallas kernels: 136 us -> 132 us
    pallas_call x1, Pallas kernels: 130 us -> 128 us  [on_device(): pl.pallas_call(kernel, out_shape=(jax.ShapeDtypeStruct((1, R), F32), jax....]
where the time goes in v3:
time: 133 us
  Pallas kernels  132 us (99%)
    pallas_call x1, Pallas kernels, on_device(): pl.pallas_call(kernel, out_shape=(jax.ShapeDtypeStruct((1, R), F32), jax....  128 us
    pallas_call x1, Pallas kernels, on_device(): pl.pallas_call(finish, grid=(2,), out_shape=(jax.ShapeDtypeStruct((R,), F...  4.35 us

profile of v3, /device:TPU:1, one launch (start us, length us, event | category | flops | bytes accessed | tf_op | source)
XLA Modules:
  0.0 132.6 jit_solution(6667555108163769865)
XLA Ops:
  0.6 127.6 %shard_map.67 = (f32[1,512]{1,0:T(1,128)}, bf16[512,1024]{1,0:T(8,128)(2,1)}, bf16[1280,1024]{1,0:T(8,128)(2,1)}) custom-call(bf16[512,1280]{1,0:T(8,128)(2,1)} %aud_hbm.1, bf16[512,1024]{1,0:T(8,128)(2,1)} %txt_hbm.1, bf16[1280,1024]{1,0:T(8,128)(2,1)} %w_hbm.1, s32[1,512]{1,0:T(1,128)} %pair_ref.1), custom_call_target="tpu_custom_call" | custom-call | flops 24000000000 | bytes 16777216 | tf_op jit(solution)/shard_map/pallas_call | solution.py:634
  128.3 4.4 %shard_map.68 = (f32[512]{0:T(512)}, bf16[512,1024]{1,0:T(8,128)(2,1)}, f32[1280,1024]{1,0:T(8,128)}) custom-call(f32[1,512]{1,0:T(1,128)} %get-tuple-element.6.loss_in, bf16[512,1024]{1,0:T(8,128)(2,1)} %get-tuple-element.7.text_in, bf16[1280,1024]{1,0:T(8,128)(2,1)} %get-tuple-element.8.proj_in), custom_call_target="tpu_custom_call" | custom-call | bytes 10485760 | tf_op jit(solution)/shard_map/pallas_call | solution.py:687

commit v4 on v3

--- a/solution.py
+++ b/solution.py
@@ -406,19 +406,22 @@
     def share_z(n):
         return remote(tfwd.at[:, part(n, 256)], gz_in.at[n], gzs.at[n], gzr.at[n], z_back)
 
-    @pl.loop(0, 4)
-    def _(n):
-        to_s, to_z = adjacent_shares(1, n, part(n, 256))
-        tfwd[:, part(n, 256)] = (gacc[1, n] + to_z).astype(BF16)
-        gacc[0, n] = gacc[0, n] + to_s
-        share_z(n).start()
-
+    def last_shares(first, last):
+        @pl.loop(first, last)
+        def _(n):
+            to_s, to_z = adjacent_shares(1, n, part(n, 256))
+            tfwd[:, part(n, 256)] = (gacc[1, n] + to_z).astype(BF16)
+            gacc[0, n] = gacc[0, n] + to_s
+            share_z(n).start()
+
+    last_shares(0, 1)
     shares_z = [share_z(n) for n in range(4)]
     started.extend(shares_z)
     for d in range(1, NX):
         weights(1, d, lse[d])
     paired_weights(1, lse[0])
     products(1)
+    last_shares(1, 2)
 
     def term_rows(which, n):
         rows = part(which, 640)
@@ -484,6 +487,7 @@
     firsts = [first_copy(n, k, d) for n in range(4) for k in range(2) for d in range(1, NX)]
     started.extend(firsts)
     started.extend(pair_copy(n) for n in range(4))
+    last_shares(2, 4)
     pass_share(0)
 
     def own_gradient(first, last):
@@ -492,7 +496,6 @@
             cols = part(n, 256)
             hacc[0:R, cols] = own_share(cols)
 
-    own_gradient(0, 2)
     for copy in firsts:
         copy.wait_recv()
     mine = (x, 4 + y)
@@ -509,7 +512,7 @@
         seconds.append(send(out2.at[0, yd], in2.at[0, d - 1], p2s.at[0, d - 1], p2r.at[0, d - 1], y_peer(d)))
         seconds.append(send(out2.at[1, xd], in2.at[1, d - 1], p2s.at[1, d - 1], p2r.at[1, d - 1], x_peer(d)))
     pass_share(1)
-    own_gradient(2, 4)
+    own_gradient(0, 1)
     for copy in seconds:
         copy.wait_recv()
     theirs = (y, x)
@@ -532,7 +535,7 @@
         zd = lax.rem(z + d, NZ)
         thirds.append(send(zb.at[zd], zin.at[d - 1], z1s.at[d - 1], z1r.at[d - 1], z_peer(d)))
     forward_share(0)
-    pass_share(2)
+    own_gradient(1, 3)
     for copy in thirds:
         copy.wait_recv()
     v = zown[z]
@@ -541,6 +544,8 @@
     zall[z] = (v * (SCALE / 256.0)).astype(BF16)
     fourths = [send(zall.at[z], zall.at[z], z2s.at[d - 1], z2r.at[d - 1], z_peer(d)) for d in far_first]
     forward_share(1)
+    pass_share(2)
+    own_gradient(3, 4)
     for copy in fourths:
         copy.wait_recv()
 
@@ -595,18 +600,18 @@
         spread(k, 5, beside(k, 1), high, ends[k][1])
     forward_share(3)
 
-    for n in range(4):
-        for k in range(2):
-            second_y[n, k].wait_recv()
-        tgrad_ref[:, n * 256:(n + 1) * 256] = (SCALE * (hacc[0:R, n * 256:(n + 1) * 256] + g_in[n].astype(F32))).astype(BF16)
-    write(tgrad_ref, tgrad_out, 16)
-
     for d, i, j in ((3, 0, 2), (1, 1, 3), (2, 4, 5)):
         for k in range(2):
             if d == 2:
                 sixths[k, i].wait_recv()
             sixths[k, j].wait_recv()
             to_sibling(beside(k, d), 4 * k + d)
+    for n in range(4):
+        for k in range(2):
+            second_y[n, k].wait_recv()
+        tgrad_ref[:, n * 256:(n + 1) * 256] = (SCALE * (hacc[0:R, n * 256:(n + 1) * 256] + g_in[n].astype(F32))).astype(BF16)
+    write(tgrad_ref, tgrad_out, 16)
+
     for copy, (p, k) in zip(lasts, blocks):
         copy.wait_recv()
         rows = pl.ds(pl.multiple_of((1 - c) * 640 + p * 80, 16), 80)

time: 133 us -> 131 us (0.985)
  Pallas kernels: 132 us -> 130 us
    pallas_call x1, Pallas kernels: 128 us -> 126 us  [on_device(): pl.pallas_call(kernel, out_shape=(jax.ShapeDtypeStruct((1, R), F32), jax....]
where the time goes in v4:
time: 131 us; the launch traced here: 130 us
  Pallas kernels  130 us (99%)
    pallas_call x1, Pallas kernels, on_device(): pl.pallas_call(kernel, out_shape=(jax.ShapeDtypeStruct((1, R), F32), jax....  126 us
    pallas_call x1, Pallas kernels, on_device(): pl.pallas_call(finish, grid=(2,), out_shape=(jax.ShapeDtypeStruct((R,), F...  4.35 us

profile of v4, /device:TPU:1, one launch (start us, length us, event | category | flops | bytes accessed | tf_op | source)
XLA Modules:
  0.0 130.5 jit_solution(14816938747121777451)
XLA Ops:
  0.6 125.5 %shard_map.67 = (f32[1,512]{1,0:T(1,128)}, bf16[512,1024]{1,0:T(8,128)(2,1)}, bf16[1280,1024]{1,0:T(8,128)(2,1)}) custom-call(bf16[512,1280]{1,0:T(8,128)(2,1)} %aud_hbm.1, bf16[512,1024]{1,0:T(8,128)(2,1)} %txt_hbm.1, bf16[1280,1024]{1,0:T(8,128)(2,1)} %w_hbm.1, s32[1,512]{1,0:T(1,128)} %pair_ref.1), custom_call_target="tpu_custom_call" | custom-call | flops 24000000000 | bytes 16777216 | tf_op jit(solution)/shard_map/pallas_call | solution.py:639
  126.1 4.4 %shard_map.68 = (f32[512]{0:T(512)}, bf16[512,1024]{1,0:T(8,128)(2,1)}, f32[1280,1024]{1,0:T(8,128)}) custom-call(f32[1,512]{1,0:T(1,128)} %get-tuple-element.6.loss_in, bf16[512,1024]{1,0:T(8,128)(2,1)} %get-tuple-element.7.text_in, bf16[1280,1024]{1,0:T(8,128)(2,1)} %get-tuple-element.8.proj_in), custom_call_target="tpu_custom_call" | custom-call | bytes 10485760 | tf_op jit(solution)/shard_map/pallas_call | solution.py:692

commit v5 on v4

--- a/solution.py
+++ b/solution.py
@@ -421,7 +421,6 @@
         weights(1, d, lse[d])
     paired_weights(1, lse[0])
     products(1)
-    last_shares(1, 2)
 
     def term_rows(which, n):
         rows = part(which, 640)
@@ -468,10 +467,10 @@
         def _():
             core_out[n] = term_rows(1 - c, n).astype(BF16)
             pair_copy(n).start()
-            sco[0, part(n, 640), :] = term_rows(c, n)
 
         @pl.when(n > 0)
         def _():
+            sco[0, part(n - 1, 640), :] = term_rows(c, n - 1)
             pair_copy(n - 1).wait_recv()
 
             @pl.loop(0, 8)
@@ -487,7 +486,7 @@
     firsts = [first_copy(n, k, d) for n in range(4) for k in range(2) for d in range(1, NX)]
     started.extend(firsts)
     started.extend(pair_copy(n) for n in range(4))
-    last_shares(2, 4)
+    last_shares(1, 4)
     pass_share(0)
 
     def own_gradient(first, last):

time: 131 us -> 132 us (level)
  no operation moved by 1% of the time
where the time goes in v5:
time: 132 us
  Pallas kernels  131 us (99%)
    pallas_call x1, Pallas kernels, on_device(): pl.pallas_call(kernel, out_shape=(jax.ShapeDtypeStruct((1, R), F32), jax....  127 us
    pallas_call x1, Pallas kernels, on_device(): pl.pallas_call(finish, grid=(2,), out_shape=(jax.ShapeDtypeStruct((R,), F...  4.35 us

profile of v5, /device:TPU:1, one launch (start us, length us, event | category | flops | bytes accessed | tf_op | source)
XLA Modules:
  0.0 131.7 jit_solution(11966823864466375409)
XLA Ops:
  0.6 126.8 %shard_map.67 = (f32[1,512]{1,0:T(1,128)}, bf16[512,1024]{1,0:T(8,128)(2,1)}, bf16[1280,1024]{1,0:T(8,128)(2,1)}) custom-call(bf16[512,1280]{1,0:T(8,128)(2,1)} %aud_hbm.1, bf16[512,1024]{1,0:T(8,128)(2,1)} %txt_hbm.1, bf16[1280,1024]{1,0:T(8,128)(2,1)} %w_hbm.1, s32[1,512]{1,0:T(1,128)} %pair_ref.1), custom_call_target="tpu_custom_call" | custom-call | flops 24000000000 | bytes 16777216 | tf_op jit(solution)/shard_map/pallas_call | solution.py:638
  127.4 4.4 %shard_map.68 = (f32[512]{0:T(512)}, bf16[512,1024]{1,0:T(8,128)(2,1)}, f32[1280,1024]{1,0:T(8,128)}) custom-call(f32[1,512]{1,0:T(1,128)} %get-tuple-element.6.loss_in, bf16[512,1024]{1,0:T(8,128)(2,1)} %get-tuple-element.7.text_in, bf16[1280,1024]{1,0:T(8,128)(2,1)} %get-tuple-element.8.proj_in), custom_call_target="tpu_custom_call" | custom-call | bytes 10485760 | tf_op jit(solution)/shard_map/pallas_call | solution.py:691
